TPU v7x, 256 devices: a whole 4x4x8 slice. The times are simulated.
256 devices in a mesh: frame: 16 (over y_lo, z), row: 16 (over y_hi, x, core).
Axes of the slice: x: 4, y: 4 (y_hi: 2, y_lo: 2; y = y_hi * 2 + y_lo), z: 8, core: 2. Of those that a mesh axis runs over, the one named last changes fastest.
Arguments:
- clip_tokens: bfloat16 [64, 32, 40, 1152], P('frame', 'row'), may hold values from -6 to 6
- modulation: float32 [6, 1152], replicated, may hold values from -3 to 3
- w_sqkv: bfloat16 [1152, 3456], P(None, 'frame'), may hold values from -1.5 to 1.5
- w_sout: bfloat16 [1152, 1152], P(None, 'frame'), may hold values from -0.1875 to 0.1875
- w_tqkv: bfloat16 [1152, 3456], P(None, 'frame'), may hold values from -1.5 to 1.5
- w_tout: bfloat16 [1152, 1152], P(None, 'frame'), may hold values from -0.1875 to 0.1875
Outputs:
- block_out: bfloat16 [64, 32, 40, 1152], P('frame', 'row')
All inputs are finite; a program needn't handle non-finite values.
Results may differ from a plain program's by a relative error of at most 0.009.
Values may be sent and summed in bfloat16 or wider, within the bound.
No kernel may reach another device: no remote copies, remote signals or barrier semaphores. Data moves between devices by JAX's collectives and lax.ppermute only.
A program may use at most 128 MiB of HBM per device.

v0:
```python
import functools
import math

import jax
import jax.numpy as jnp
from jax import lax
from jax.experimental import pallas as pl
from jax.experimental.pallas import tpu as pltpu
from jax.sharding import PartitionSpec as P

HEADS = 16
HEAD_DIM = 72
D = 1152
GROUP = 4 * HEAD_DIM
PAD = 80
BF = jnp.bfloat16
F32 = jnp.float32
SCALE = math.log2(math.e) / math.sqrt(HEAD_DIM)
VMEM = pl.BlockSpec(memory_space=pltpu.VMEM)
ANY = pl.BlockSpec(memory_space=pl.ANY)
NT = (((1,), (1,)), ((), ()))


def params(mib):
    return pltpu.CompilerParams(vmem_limit_bytes=mib * 1024 * 1024)


def normalize(inputs, shift, scale):
    average = jnp.mean(inputs, axis=-1, keepdims=True)
    centered = inputs - average
    variance = jnp.mean(centered * centered, axis=-1, keepdims=True)
    return (centered * lax.rsqrt(variance + 1e-06) * (1.0 + scale) + shift).astype(BF)


def place():
    r = lax.axis_index("row")
    return r >> 3, (r >> 1) & 3, r & 1


def norm_kernel(clip_ref, mod_ref, keep_ref, swap_ref, give_ref):
    yh, _, c = place()

    def normed(j):
        return normalize(clip_ref[j].astype(F32), mod_ref[0:1, :], mod_ref[1:2, :])

    keep_ref[...] = normed(2 * yh + c)
    swap_ref[...] = normed(2 * yh + 1 - c)
    for i in range(2):
        give_ref[i] = normed(2 * (1 - yh) + i)


def prepare_kernel(qkv_ref, sout_ref, tout_ref, proj_ref, out_ref):
    c = lax.axis_index("row") & 1
    for core, (lo, mid, width, proj) in enumerate(((0, 144, 40, sout_ref), (72, 184, 32, tout_ref))):

        @pl.when(c == core)
        def _(lo=lo, mid=mid, width=width, proj=proj):
            w = qkv_ref[...].astype(F32)
            rows = [w[lo : lo + 72], jnp.zeros((8, D), F32), w[mid : mid + width], jnp.zeros((48 - width, D), F32)]
            out_ref[...] = jnp.concatenate(rows, axis=0).astype(BF)
            proj_ref[...] = proj[...]


def repack_kernel(w_ref, out_ref):
    _, x, _ = place()
    for g in range(4):

        @pl.when(x == g)
        def _(g=g):
            cols = []
            for part in range(3):
                for h in range(4):
                    p = 16 * part + 4 * g + h
                    cols.append(w_ref[p // 3, :, 72 * (p % 3) : 72 * (p % 3) + 72])
            block = jnp.concatenate(cols, axis=1)
            block = jnp.concatenate([block, jnp.zeros((4, 3 * GROUP), BF)], axis=0)
            for f in range(16):
                out_ref[f] = block


def launch(pairs, sems):
    copies = [pltpu.make_async_copy(src, dst, sems.at[i]) for i, (src, dst) in enumerate(pairs)]
    for copy in copies:
        copy.start()
    return copies


def spatial_kernel(*refs):
    tokens, (w0, w1, o_ref, x_scr, w_in, w_scr, q_scr, k_scr, v_scr, out_scr, in_sems, out_sems) = refs[:8], refs[8:]
    yh, x, c = place()
    pairs = [(w, w_in.at[s]) for s, w in enumerate((w0, w1))]
    pairs += [(ref, x_scr.at[pl.ds(160 * i, 160)]) for i, ref in enumerate(tokens)]
    for s, copy in enumerate(launch(pairs, in_sems)[:2]):
        copy.wait()
        rows = pl.ds(pl.multiple_of(576 * (c ^ s), 64), 576)
        w_scr[rows, :] = jnp.concatenate([w_in[s, i, :36] for i in range(16)], axis=0)
    lane = lax.broadcasted_iota(jnp.int32, (320, 128 - HEAD_DIM), 1)
    zeros = jnp.zeros((320, 128 - HEAD_DIM), BF)
    ones = jnp.where(lane == 0, 1.0, 0.0).astype(BF)
    def project(i, carry):
        for near in range(2):
            half = x_scr.at[pl.ds(pl.multiple_of(320 * i + 160 * near, 32), 160)]
            pltpu.make_async_copy(tokens[0], half, in_sems.at[2 + 2 * i + near]).wait()
        rows = pl.ds(pl.multiple_of(320 * i, 64), 320)
        qkv = jnp.dot(x_scr[rows, :], w_scr[...], preferred_element_type=F32)
        for h in range(4):
            lo = 72 * h
            q = (qkv[:, lo : lo + 72] * SCALE).astype(BF)
            k = qkv[:, GROUP + lo : GROUP + lo + 72].astype(BF)
            v = qkv[:, 2 * GROUP + lo : 2 * GROUP + lo + 72].astype(BF)
            q_scr[h, rows, :] = jnp.concatenate([q, zeros], axis=1)
            k_scr[h, rows, :] = jnp.concatenate([k, zeros], axis=1)
            v_scr[h, rows, :] = jnp.concatenate([v, ones], axis=1)
        return carry

    lax.fori_loop(0, 4, project, 0)

    def outgoing(i, t):
        dest = (yh ^ (t >> 1)) * 8 + ((x - i) & 3) * 2 + (c ^ (t & 1))
        return pltpu.make_async_copy(out_scr.at[i, pl.ds(80 * t, 80)], o_ref.at[dest], out_sems.at[i, t])

    def step(i, carry):
        heads = []
        for h in range(4):
            q = q_scr[h, pl.ds(pl.multiple_of(320 * i, 64), 320), :]
            s = lax.dot_general(q, k_scr[h], NT, preferred_element_type=F32)
            m = jnp.max(s, axis=-1, keepdims=True)
            p = jnp.exp2(s - m).astype(BF)
            o = jnp.dot(p, v_scr[h], preferred_element_type=F32)
            heads.append((o[:, :72] / o[:, 72:73]).astype(BF))
        out_scr[i] = jnp.concatenate(heads, axis=1)
        for t in range(4):
            outgoing(i, t).start()
        return carry

    lax.fori_loop(0, 4, step, 0)
    for i in range(4):
        for t in range(4):
            outgoing(i, t).wait()


def spread(frame_major):
    if frame_major:
        row = lax.broadcasted_iota(jnp.int32, (512, 320), 0)
        col = lax.broadcasted_iota(jnp.int32, (512, 320), 1)
    else:
        row = lax.broadcasted_iota(jnp.int32, (320, 512), 1)
        col = lax.broadcasted_iota(jnp.int32, (320, 512), 0)
    f, t = row >> 5, row & 31
    j = (t * 13) >> 6
    want = 80 * j + 5 * f + (t - 5 * j)
    return jnp.where((t < 20) & (col == want), 1.0, 0.0).astype(BF)


def compact(narrow):
    if narrow:
        wide = lax.broadcasted_iota(jnp.int32, (320, 512), 1)
        thin = lax.broadcasted_iota(jnp.int32, (320, 512), 0)
    else:
        wide = lax.broadcasted_iota(jnp.int32, (512, 320), 0)
        thin = lax.broadcasted_iota(jnp.int32, (512, 320), 1)
    f, t = wide >> 5, wide & 31
    j = (t * 13) >> 6
    return jnp.where((t < 20) & (thin == 64 * (t - 5 * j) + 4 * f + j), 1.0, 0.0).astype(BF)


def unpack_chunks(ref, scr):
    zeros = jnp.zeros((8, D), BF)
    for f in range(16):
        scr[32 * f : 32 * f + 32, :] = jnp.concatenate([ref[f], zeros], axis=0)
    return scr[...]


def fetch_projection(core, mine, other, w_scr, sems):
    c = lax.axis_index("row") & 1
    y_lo = lax.axis_index("frame") >> 3

    def pairs(refs):
        first = pl.multiple_of(576 * y_lo, 64)
        second = pl.multiple_of(576 * (1 - y_lo), 64)
        places = (pl.ds(first, 576), pl.ds(second, 288), pl.ds(second + 288, 288))
        return [(ref, w_scr.at[rows]) for ref, rows in zip(refs, places)]

    for cond, refs in ((c == core, mine), (c != core, other)):

        @pl.when(cond)
        def _(refs=refs):
            launch(pairs(refs), sems)

    return [pltpu.make_async_copy(src, dst, sems.at[i]) for i, (src, dst) in enumerate(pairs(mine))]


def middle_kernel(o_in, clip_in, mod_ref, m0, m1, m2, n0, n1, n2, mid_out, out_ref, o_ref, clip_ref, mid_ref, w_scr, sems, w_sems):
    copies = launch([(o_in, o_ref), (clip_in, clip_ref)], sems)
    weights = fetch_projection(0, (m0, m1, m2), (n0, n1, n2), w_scr, w_sems)
    copies[0].wait()
    groups = [
        jnp.concatenate([o_ref[8 * (j >> 1) + 2 * g + (j & 1)] for j in range(4)], axis=0) for g in range(4)
    ]
    o = jnp.concatenate(groups, axis=1)
    for copy in weights:
        copy.wait()
    total = lax.dot_general(o, w_scr[...], NT, preferred_element_type=F32)
    copies[1].wait()
    mid = clip_ref[...].astype(F32) + mod_ref[2:3, :] * total
    mid_ref[...] = mid
    keep = pltpu.make_async_copy(mid_ref, mid_out, sems.at[2])
    keep.start()
    normed = normalize(mid, mod_ref[3:4, :], mod_ref[4:5, :])
    out = jnp.dot(spread(True), normed, preferred_element_type=F32).astype(BF)
    for f in range(16):
        out_ref[f] = out[32 * f : 32 * f + 24]
    keep.wait()


def temporal_kernel(x_ref, *refs):
    weights, (o_ref, y_scr, scr) = refs[:6], refs[6:]
    c = lax.axis_index("row") & 1
    y_lo = lax.axis_index("frame") >> 3
    x = jnp.dot(compact(True), unpack_chunks(x_ref, scr), preferred_element_type=F32).astype(BF)
    for t in range(2):
        y = [lax.dot_general(x, w[...], NT, preferred_element_type=F32) for w in weights[3 * t : 3 * t + 3]]
        y_scr[y_lo, c ^ t] = y[0]
        y_scr[1 - y_lo, c ^ t] = jnp.concatenate(y[1:], axis=1)

    def part(p):
        i, sub = p // 3, p % 3
        lo = 128 * (i % 8)
        if sub < 2:
            return y_scr[i // 8, sub, :, lo : lo + PAD]
        return jnp.concatenate([y_scr[i // 8, core, :, lo + 80 : lo + 120] for core in range(2)], axis=1)

    row = lax.broadcasted_iota(jnp.int32, (320, 320), 0)
    col = lax.broadcasted_iota(jnp.int32, (320, 320), 1)
    same = (row >> 6) == (col >> 6)
    heads = []
    for h in range(HEADS):
        q = (part(h) * SCALE).astype(BF)
        k = part(16 + h).astype(BF)
        v = part(32 + h).astype(BF)
        s = lax.dot_general(q, k, NT, preferred_element_type=F32)
        s = jnp.where(same, s, -1e30)
        m = jnp.max(s, axis=-1, keepdims=True)
        p = jnp.exp2(s - m)
        total = jnp.sum(p, axis=-1, keepdims=True)
        o = jnp.dot(p.astype(BF), v, preferred_element_type=F32) / total
        heads.append(o[:, :72].astype(BF))
    o = jnp.concatenate(heads, axis=1)
    out = jnp.dot(compact(False), o, preferred_element_type=F32).astype(BF)
    for f in range(16):
        o_ref[f] = out[32 * f : 32 * f + 24]


def final_kernel(o_in, mid_in, mod_ref, m0, m1, m2, n0, n1, n2, out_ref, o_ref, mid_ref, w_scr, scr, sems, w_sems):
    copies = launch([(mid_in, mid_ref), (o_in, o_ref)], sems)
    weights = fetch_projection(1, (m0, m1, m2), (n0, n1, n2), w_scr, w_sems)
    copies[1].wait()
    o = jnp.dot(spread(False), unpack_chunks(o_ref, scr), preferred_element_type=F32).astype(BF)
    for copy in weights:
        copy.wait()
    y = lax.dot_general(o, w_scr[...], NT, preferred_element_type=F32)
    copies[0].wait()
    out_ref[...] = (mid_ref[...] + mod_ref[5:6, :] * y).astype(BF)


def shift_x(value, d):
    pairs = [(r, (r & 9) | ((((r >> 1) + d) & 3) << 1)) for r in range(16)]
    return lax.ppermute(value, "row", pairs)


def swap_core(value):
    return lax.ppermute(value, "row", [(r, r ^ 1) for r in range(16)])


def swap_yh(value):
    return lax.ppermute(value, "row", [(r, r ^ 8) for r in range(16)])


def halves(value):
    half = value.shape[0] // 2
    return value[:half], value[half:]


def from_y_neighbours(parts):
    got = []
    for part, flip in zip(parts, (0, 8)):
        pairs = [(16 * f + r, 16 * (f ^ 8) + (r ^ flip)) for f in range(16) for r in range(16)]
        got.append(lax.ppermute(part, ("frame", "row"), pairs))
    return got


def gather_half(value):
    rings = [list(range(8)), list(range(8, 16))]
    return lax.all_gather(value, "frame", axis=0, tiled=True, axis_index_groups=rings)


def call(kernel, outs, n_in, scratch=(), mib=56, any_in=(), any_out=(), us=2):
    return pl.pallas_call(
        kernel,
        out_shape=outs,
        in_specs=[ANY if i in any_in else VMEM for i in range(n_in)],
        out_specs=[ANY if i in any_out else VMEM for i in range(len(outs))] if isinstance(outs, tuple) else ANY if any_out else VMEM,
        scratch_shapes=list(scratch),
        compiler_params=params(mib),
        cost_estimate=pl.CostEstimate(flops=us * 10**9, bytes_accessed=us * 10**6, transcendentals=0),
    )


def sds(shape, dtype=BF):
    return jax.ShapeDtypeStruct(shape, dtype)


def on_device(clip_tokens, modulation, w_sqkv, w_sout, w_tqkv, w_tout):
    frames_here, rows_here, patches, features = clip_tokens.shape
    tokens = rows_here * patches
    yh, x, c = place()

    proj, tq = call(prepare_kernel, (sds((72, D)), sds((128, D))), 3, mib=60)(w_tqkv.T, w_sout.T, w_tout.T)
    proj = gather_half(proj)
    tq = gather_half(tq)

    clip = clip_tokens.reshape(frames_here, tokens, features)
    keep, swap, give = call(norm_kernel, (sds((80, D)), sds((80, D)), sds((2, 80, D))), 2, mib=12)(clip, modulation)
    first = lax.dynamic_slice(w_sqkv, (576 * c, 0), (576, 216))
    keep, swap, give, first = lax.optimization_barrier((keep, swap, give, first))

    theirs = swap_yh(give)
    own = jnp.concatenate([keep, swap_core(swap)], axis=0)
    own, first = lax.optimization_barrier((own, first))
    first = lax.all_to_all(first.reshape(16, 36, 216), "frame", 0, 0, tiled=True)
    near = {d: shift_x(own, d) for d in (1, 3)}
    second = call(repack_kernel, sds((16, 40, 3 * GROUP)), 1, mib=12)(first)
    far = {}
    far[0] = jnp.concatenate([theirs[c], swap_core(theirs[1 - c])], axis=0)
    near[1], near[3], own, far[0], second = lax.optimization_barrier((near[1], near[3], own, far[0], second))
    near[0] = own
    near[2] = shift_x(own, 2)
    for d in (1, 2, 3):
        far[d] = shift_x(far[0], d)
    second = lax.all_to_all(second, "frame", 0, 0, tiled=True)
    _, proj = lax.optimization_barrier((near[2], proj))
    proj = [proj] + from_y_neighbours(halves(proj))
    near[2], far[1], far[2], far[3], second = lax.optimization_barrier((near[2], far[1], far[2], far[3], second))
    w_other = swap_core(second)

    o_s = call(
        spatial_kernel,
        sds((16, tokens, GROUP)),
        10,
        scratch=[
            pltpu.VMEM((1280, D), BF),
            pltpu.VMEM((2, 16, 40, 3 * GROUP), BF),
            pltpu.VMEM((D, 3 * GROUP), BF),
            pltpu.VMEM((4, 1280, 128), BF),
            pltpu.VMEM((4, 1280, 128), BF),
            pltpu.VMEM((4, 1280, 128), BF),
            pltpu.VMEM((4, 320, GROUP), BF),
            pltpu.SemaphoreType.DMA((10,)),
            pltpu.SemaphoreType.DMA((4, 4)),
        ],
        any_in=range(10),
        any_out=(0,),
        mib=52,
        us=15,
    )(*[half[d] for d in range(4) for half in (near, far)], second, w_other)
    o_s, *proj = lax.optimization_barrier((o_s, *proj))
    proj_other = [swap_core(v) for v in proj]
    o_s = lax.all_to_all(o_s, "row", 0, 0, tiled=True)
    _, tq, *parts = lax.optimization_barrier((o_s, tq, *halves(tq)))
    tq = [tq] + from_y_neighbours(parts)

    mid, chunks = call(
        middle_kernel,
        (sds((320, D), F32), sds((16, 24, D))),
        9,
        scratch=[
            pltpu.VMEM((16, tokens, GROUP), BF),
            pltpu.VMEM((320, D), BF),
            pltpu.VMEM((320, D), F32),
            pltpu.VMEM((D, D), BF),
            pltpu.SemaphoreType.DMA((3,)),
            pltpu.SemaphoreType.DMA((3,)),
        ],
        any_in=(0, 1, 3, 4, 5, 6, 7, 8),
        any_out=(0,),
        mib=60,
        us=4,
    )(o_s, clip.reshape(320, D), modulation, *proj, *proj_other)
    _, tq[0] = lax.optimization_barrier((chunks, tq[0]))
    tq_other = [swap_core(v) for v in tq]
    chunks = lax.all_to_all(chunks, "frame", 0, 0, tiled=True)

    o_t = call(
        temporal_kernel,
        sds((16, 24, D)),
        7,
        scratch=[pltpu.VMEM((2, 2, 320, 1024), F32), pltpu.VMEM((512, D), BF)],
        mib=40,
        us=12,
    )(chunks, *tq, *tq_other)
    o_t = lax.all_to_all(o_t, "frame", 0, 0, tiled=True)
    out = call(
        final_kernel,
        sds((320, D)),
        9,
        scratch=[
            pltpu.VMEM((16, 24, D), BF),
            pltpu.VMEM((320, D), F32),
            pltpu.VMEM((D, D), BF),
            pltpu.VMEM((512, D), BF),
            pltpu.SemaphoreType.DMA((2,)),
            pltpu.SemaphoreType.DMA((3,)),
        ],
        any_in=(0, 1, 3, 4, 5, 6, 7, 8),
        mib=60,
        us=4,
    )(o_t, mid, modulation, *proj, *proj_other)
    return out.reshape(frames_here, rows_here, patches, features)


def solution(mesh):
    in_specs = (
        P("frame", "row", None, None),
        P(),
        P(None, "frame"),
        P(None, "frame"),
        P(None, "frame"),
        P(None, "frame"),
    )
    out_specs = P("frame", "row", None, None)
    return jax.shard_map(
        on_device, mesh=mesh, in_specs=in_specs, out_specs=out_specs, check_vma=False
    )
```

profile of v0, /device:TPU:32, one launch (start us, length us, event | category | flops | bytes accessed | tf_op | source)
XLA Modules:
  0.0 222.3 jit_solution(10496835536651412727)
XLA Ops:
  6.5 1.0 copy-done
  7.6 0.2 constant_dynamic-slice_fusion
  7.7 0.0 copy-start.2
  7.7 1.1 copy-done.2
  8.8 0.8 copy-done.3
  9.6 0.5 shard_map.64
  10.2 0.1 collective-permute-start
  10.3 3.3 %collective-permute-start.3 = (bf16[2,80,1152]{2,1,0:T(8,128)(2,1)S(1)}, bf16[2,80,1152]{2,1,0:T(8,128)(2,1)S(1)}, u32[]{:S(2)}, u32[]{:S(2)}) collective-permute-start(bf16[2,80,1152]{2,1,0:T(8,128)(2,1)S(1)} %get-tuple-element.44), channel_id=1, source_target_pairs={{0,8},{1,9},{2,10},{3,11},{4,12},{5,13},{6,14},{7,15},{8,0},{9,1},... | collective-permute-start | bytes 1105928 | tf_op jit(solution)/shard_map/ppermute | solution.py:276
  13.5 2.0 shard_map.67
  15.5 0.0 all-gather.3.cloned.1.call-update
  15.5 0.0 collective-permute-done
  15.6 0.2 copy.8
  15.7 0.8 reshape.10
  16.5 8.7 %all-to-all-start = ((bf16[16,36,216]{2,1,0:T(8,128)(2,1)}), bf16[16,36,216]{2,1,0:T(8,128)(2,1)S(1)}, u32[]{:S(2)}, u32[]{:S(2)}) async-start(bf16[16,36,216]{2,1,0:T(8,128)(2,1)} %reshape.10), calls=%async_computation | async-start | bytes 655360 | tf_op jit(solution)/shard_map/all_to_all | solution.py:330
  25.2 0.0 collective-permute-done.3
  25.3 0.1 collective-permute-start.4
  25.4 2.8 %collective-permute-start.2 = (bf16[160,1152]{1,0:T(8,128)(2,1)S(1)}, bf16[160,1152]{1,0:T(8,128)(2,1)S(1)}, u32[]{:S(2)}, u32[]{:S(2)}) collective-permute-start(bf16[160,1152]{1,0:T(8,128)(2,1)S(1)} %pad_maximum_fusion.refs_0_), channel_id=1, source_target_pairs={{0,6},{1,7},{2,0},{3,1},{4,2},{5,3},{6,4},{7,5},{8,14},{9,15},{10,... | collective-permute-start | bytes 1105928 | tf_op jit(solution)/shard_map/ppermute | solution.py:268
  28.2 0.0 collective-permute-start.1
  28.3 10.8 %all-to-all-done.w_ref = bf16[16,36,216]{2,1,0:T(8,128)(2,1)S(1)} async-done(((bf16[16,36,216]{2,1,0:T(8,128)(2,1)}), bf16[16,36,216]{2,1,0:T(8,128)(2,1)S(1)}, u32[]{:S(2)}, u32[]{:S(2)}) %all-to-all-start) | async-done | bytes 248864 | tf_op jit(solution)/shard_map/all_to_all | solution.py:330
  39.0 1.2 shard_map.65
  40.2 0.0 collective-permute-done.2.refs_6_
  40.2 0.0 collective-permute-done.1.refs_2_
  40.2 8.0 %all-to-all-start.1 = ((bf16[16,40,864]{2,1,0:T(8,128)(2,1)}), bf16[16,40,864]{2,1,0:T(8,128)(2,1)}, u32[]{:S(2)}, u32[]{:S(2)}) async-start(bf16[16,40,864]{2,1,0:T(8,128)(2,1)} %shard_map.65), calls=%async_computation.1 | async-start | bytes 2293760 | tf_op jit(solution)/shard_map/all_to_all | solution.py:340
  48.2 0.0 all-gather.5.cloned.1.call-start
  48.3 0.7 all-gather.5.cloned.1.call-update
  49.0 0.8 collective-permute-start.5
  49.8 1.1 collective-permute-start.8
  50.9 1.7 collective-permute-start.7
  52.6 1.4 collective-permute-start.6
  54.0 8.2 %collective-permute-done.5.refs_4_ = bf16[160,1152]{1,0:T(8,128)(2,1)S(1)} collective-permute-done((bf16[160,1152]{1,0:T(8,128)(2,1)S(1)}, bf16[160,1152]{1,0:T(8,128)(2,1)S(1)}, u32[]{:S(2)}, u32[]{:S(2)}) %collective-permute-start.5) | collective-permute-done | bytes 368672 | tf_op jit(solution)/shard_map/ppermute | solution.py:268
  62.2 5.6 %collective-permute-done.8.refs_7_ = bf16[160,1152]{1,0:T(8,128)(2,1)S(1)} collective-permute-done((bf16[160,1152]{1,0:T(8,128)(2,1)S(1)}, bf16[160,1152]{1,0:T(8,128)(2,1)S(1)}, u32[]{:S(2)}, u32[]{:S(2)}) %collective-permute-start.8) | collective-permute-done | bytes 368672 | tf_op jit(solution)/shard_map/ppermute | solution.py:268
  67.8 2.2 collective-permute-done.7.refs_5_
  70.0 0.7 copy-done.12
  70.8 5.0 %collective-permute-done.6.refs_3_ = bf16[160,1152]{1,0:T(8,128)(2,1)S(1)} collective-permute-done((bf16[160,1152]{1,0:T(8,128)(2,1)S(1)}, bf16[160,1152]{1,0:T(8,128)(2,1)S(1)}, u32[]{:S(2)}, u32[]{:S(2)}) %collective-permute-start.6) | collective-permute-done | bytes 368672 | tf_op jit(solution)/shard_map/ppermute | solution.py:268
  75.7 3.0 %all-to-all-done.1.refs_8_ = bf16[16,40,864]{2,1,0:T(8,128)(2,1)} async-done(((bf16[16,40,864]{2,1,0:T(8,128)(2,1)}), bf16[16,40,864]{2,1,0:T(8,128)(2,1)}, u32[]{:S(2)}, u32[]{:S(2)}) %all-to-all-start.1) | async-done | bytes 1105952 | tf_op jit(solution)/shard_map/all_to_all | solution.py:340
  78.7 1.4 fusion.1
  80.1 1.6 collective-permute-start.11
  81.8 0.0 collective-permute-start.10
  81.8 0.0 collective-permute-done.9.refs_9_
  81.8 1.0 copy-done.6
  82.8 17.7 %shard_map.66 = bf16[16,80,288]{2,1,0:T(8,128)(2,1)} custom-call(bf16[160,1152]{1,0:T(8,128)(2,1)S(1)} %pad_maximum_fusion.refs_0_, bf16[160,1152]{1,0:T(8,128)(2,1)S(1)} %pad_maximum_fusion.1.refs_1_, bf16[160,1152]{1,0:T(8,128)(2,1)S(1)} %collective-permute-done.1.refs_2_, bf16[160,1152]{1,0:T(8,128)(2,1)S(1)} %collective-permute-done.6.refs_3_, ...), custom_call_target="tpu_custom_call" | custom-call | flops 15000000512 | bytes 15000000 | tf_op jit(solution)/shard_map/pallas_call | solution.py:346
  100.5 0.0 collective-permute-done.11.m2
  100.5 0.8 copy-done.7
  101.4 0.9 copy-done.9
  102.2 0.2 collective-permute-start.12
  102.5 6.5 %all-to-all-start.2 = ((bf16[16,80,288]{2,1,0:T(8,128)(2,1)}), bf16[16,80,288]{2,1,0:T(8,128)(2,1)S(1)}, u32[]{:S(2)}, u32[]{:S(2)}) async-start(bf16[16,80,288]{2,1,0:T(8,128)(2,1)} %shard_map.66), calls=%async_computation.2 | async-start | bytes 1966080 | tf_op jit(solution)/shard_map/all_to_all | solution.py:368
  109.0 0.4 collective-permute-start.13
  109.4 0.2 collective-permute-start.14
  109.6 1.0 all-gather.5.cloned.1.call-done.refs_0_
  110.6 3.2 %fusion = (bf16[512,1152]{1,0:T(8,128)(2,1)}, bf16[512,1152]{1,0:T(8,128)(2,1)}) fusion(bf16[1024,1152]{1,0:T(8,128)(2,1)} %all-gather.5.cloned.1.call-done.refs_0_), kind=kLoop, calls=%fused_computation.5 | loop fusion | bytes 4718592 | tf_op jit(solution)/shard_map/slice | solution.py:281
  113.8 12.5 %all-to-all-done.2.o_in = bf16[16,80,288]{2,1,0:T(8,128)(2,1)S(1)} async-done(((bf16[16,80,288]{2,1,0:T(8,128)(2,1)}), bf16[16,80,288]{2,1,0:T(8,128)(2,1)S(1)}, u32[]{:S(2)}, u32[]{:S(2)}) %all-to-all-start.2) | async-done | bytes 737312 | tf_op jit(solution)/shard_map/all_to_all | solution.py:368
  126.3 1.1 collective-permute-start.16
  127.4 1.1 copy-done.5
  128.5 7.0 %shard_map.68 = (f32[320,1152]{1,0:T(8,128)}, bf16[16,24,1152]{2,1,0:T(8,128)(2,1)}) custom-call(bf16[16,80,288]{2,1,0:T(8,128)(2,1)} %copy-done.4, bf16[320,1152]{1,0:T(8,128)(2,1)} %bitcast.10, f32[6,1152]{1,0:T(8,128)} %mod_ref.5, bf16[576,1152]{1,0:T(8,128)(2,1)} %all-gather.3.cloned.1.call-done.m0, bf16[288,1152]{1,0:T(8,128)(2,1)} %copy-done.9, ...), custom_call_target="tpu_custom_call" | custom-call | flops 4000000000 | bytes 4000000 | tf_op jit(solution)/shard_map/pallas_call | solution.py:372
  135.5 0.1 collective-permute-start.17
  135.6 4.7 %all-to-all-start.3 = ((bf16[16,24,1152]{2,1,0:T(8,128)(2,1)}), bf16[16,24,1152]{2,1,0:T(8,128)(2,1)}, u32[]{:S(2)}, u32[]{:S(2)}) async-start(bf16[16,24,1152]{2,1,0:T(8,128)(2,1)} %get-tuple-element.62), calls=%async_computation.3 | async-start | bytes 1769472 | tf_op jit(solution)/shard_map/all_to_all | solution.py:391
  140.4 21.9 %collective-permute-done.15.refs_1_ = bf16[512,1152]{1,0:T(8,128)(2,1)} collective-permute-done((bf16[512,1152]{1,0:T(8,128)(2,1)}, bf16[512,1152]{1,0:T(8,128)(2,1)}, u32[]{:S(2)}, u32[]{:S(2)}) %collective-permute-start.15) | collective-permute-done | bytes 1179680 | tf_op jit(solution)/shard_map/ppermute | solution.py:288
  162.3 0.5 collective-permute-start.19
  162.8 1.3 all-to-all-done.3.x_ref
  164.1 1.4 collective-permute-done.18.refs_4_
  165.5 1.7 collective-permute-done.19.refs_5_
  167.2 14.0 %shard_map.69 = bf16[16,24,1152]{2,1,0:T(8,128)(2,1)S(1)} custom-call(bf16[16,24,1152]{2,1,0:T(8,128)(2,1)} %all-to-all-done.3.x_ref, bf16[1024,1152]{1,0:T(8,128)(2,1)S(1)} %copy-done.1, bf16[512,1152]{1,0:T(8,128)(2,1)} %collective-permute-done.15.refs_1_, bf16[512,1152]{1,0:T(8,128)(2,1)} %collective-permute-done.16.refs_2_, ...), custom_call_target="tpu_custom_call" | custom-call | flops 12000000000 | bytes 12000000 | tf_op jit(solution)/shard_map/pallas_call | solution.py:393
  181.2 28.7 %all_to_all.25.o_in = bf16[16,24,1152]{2,1,0:T(8,128)(2,1)} all-to-all(bf16[16,24,1152]{2,1,0:T(8,128)(2,1)S(1)} %shard_map.69), channel_id=1, replica_groups=mesh['frame'=16,'row'=16] {'frame'}, dimensions={0} | all-to-all | bytes 1769472 | tf_op jit(solution)/shard_map/all_to_all | solution.py:401
  209.9 5.5 %shard_map.70 = bf16[320,1152]{1,0:T(8,128)(2,1)} custom-call(bf16[16,24,1152]{2,1,0:T(8,128)(2,1)} %all_to_all.25.o_in, f32[320,1152]{1,0:T(8,128)} %get-tuple-element.68.mid_in, f32[6,1152]{1,0:T(8,128)} %mod_ref.5, bf16[576,1152]{1,0:T(8,128)(2,1)} %all-gather.3.cloned.1.call-done.m0, bf16[288,1152]{1,0:T(8,128)(2,1)} %copy-done.9, ...), custom_call_target="tpu_custom_call" | custom-call | flops 4000000000 | bytes 4000000 | tf_op jit(solution)/shard_map/pallas_call | solution.py:402
  (32 shorter events, 0.2 us)
Async XLA Ops:
  6.5 1.0 copy-start
  6.5 72.2 %all-gather.3.cloned.1.call-start = ((), (), s32[]{:S(2)}) async-start(), calls=%async_computation.5 | async-start | bytes 1492992 | tf_op jit(solution)/shard_map/all_gather | solution.py:294
  7.7 1.1 copy-start.2
  8.8 0.8 copy-start.3
  10.2 5.4 %collective-permute-start = (bf16[80,1152]{1,0:T(8,128)(2,1)S(1)}, bf16[80,1152]{1,0:T(8,128)(2,1)S(1)}, u32[]{:S(2)}, u32[]{:S(2)}) collective-permute-start(bf16[80,1152]{1,0:T(8,128)(2,1)S(1)} %get-tuple-element.41), channel_id=1, source_target_pairs={{0,1},{1,0},{2,3},{3,2},{4,5},{5,4},{6,7},{7,6},{8,9},{9,8},{10,11... | collective-permute-start | bytes 552968 | tf_op jit(solution)/shard_map/ppermute | solution.py:272
  10.3 15.0 %collective-permute-start.3 = (bf16[2,80,1152]{2,1,0:T(8,128)(2,1)S(1)}, bf16[2,80,1152]{2,1,0:T(8,128)(2,1)S(1)}, u32[]{:S(2)}, u32[]{:S(2)}) collective-permute-start(bf16[2,80,1152]{2,1,0:T(8,128)(2,1)S(1)} %get-tuple-element.44), channel_id=1, source_target_pairs={{0,8},{1,9},{2,10},{3,11},{4,12},{5,13},{6,14},{7,15},{8,0},{9,1},... | collective-permute-start | bytes 1105928 | tf_op jit(solution)/shard_map/ppermute | solution.py:276
  16.5 22.5 %all-to-all-start = ((bf16[16,36,216]{2,1,0:T(8,128)(2,1)}), bf16[16,36,216]{2,1,0:T(8,128)(2,1)S(1)}, u32[]{:S(2)}, u32[]{:S(2)}) async-start(bf16[16,36,216]{2,1,0:T(8,128)(2,1)} %reshape.10), calls=%async_computation | async-start | bytes 655360 | tf_op jit(solution)/shard_map/all_to_all | solution.py:330
  25.3 2.9 %collective-permute-start.4 = (bf16[80,1152]{1,0:T(8,128)(2,1)S(1)}, bf16[80,1152]{1,0:T(8,128)(2,1)S(1)}, u32[]{:S(2)}, u32[]{:S(2)}) collective-permute-start(bf16[80,1152]{1,0:T(8,128)(2,1)S(1)} %get-tuple-element.74), channel_id=1, source_target_pairs={{0,1},{1,0},{2,3},{3,2},{4,5},{5,4},{6,7},{7,6},{8,9},{9,8},{10,11... | collective-permute-start | bytes 552968 | tf_op jit(solution)/shard_map/ppermute | solution.py:272
  25.4 14.8 %collective-permute-start.2 = (bf16[160,1152]{1,0:T(8,128)(2,1)S(1)}, bf16[160,1152]{1,0:T(8,128)(2,1)S(1)}, u32[]{:S(2)}, u32[]{:S(2)}) collective-permute-start(bf16[160,1152]{1,0:T(8,128)(2,1)S(1)} %pad_maximum_fusion.refs_0_), channel_id=1, source_target_pairs={{0,6},{1,7},{2,0},{3,1},{4,2},{5,3},{6,4},{7,5},{8,14},{9,15},{10,... | collective-permute-start | bytes 1105928 | tf_op jit(solution)/shard_map/ppermute | solution.py:268
  28.2 12.0 %collective-permute-start.1 = (bf16[160,1152]{1,0:T(8,128)(2,1)S(1)}, bf16[160,1152]{1,0:T(8,128)(2,1)S(1)}, u32[]{:S(2)}, u32[]{:S(2)}) collective-permute-start(bf16[160,1152]{1,0:T(8,128)(2,1)S(1)} %pad_maximum_fusion.refs_0_), channel_id=1, source_target_pairs={{0,2},{1,3},{2,4},{3,5},{4,6},{5,7},{6,0},{7,1},{8,10},{9,11},{10,... | collective-permute-start | bytes 1105928 | tf_op jit(solution)/shard_map/ppermute | solution.py:268
  40.2 8.7 %copy-start.10 = (bf16[160,1152]{1,0:T(8,128)(2,1)}, bf16[160,1152]{1,0:T(8,128)(2,1)S(1)}, u32[]{:S(2)}) copy-start(bf16[160,1152]{1,0:T(8,128)(2,1)S(1)} %collective-permute-done.2.refs_6_) | copy-start | bytes 1105924
  40.2 38.5 %all-to-all-start.1 = ((bf16[16,40,864]{2,1,0:T(8,128)(2,1)}), bf16[16,40,864]{2,1,0:T(8,128)(2,1)}, u32[]{:S(2)}, u32[]{:S(2)}) async-start(bf16[16,40,864]{2,1,0:T(8,128)(2,1)} %shard_map.65), calls=%async_computation.1 | async-start | bytes 2293760 | tf_op jit(solution)/shard_map/all_to_all | solution.py:340
  48.2 62.3 %all-gather.5.cloned.1.call-start = ((), (), s32[]{:S(2)}) async-start(), calls=%async_computation.6 | async-start | bytes 2654208 | tf_op jit(solution)/shard_map/all_gather | solution.py:294
  49.0 13.2 %collective-permute-start.5 = (bf16[160,1152]{1,0:T(8,128)(2,1)S(1)}, bf16[160,1152]{1,0:T(8,128)(2,1)S(1)}, u32[]{:S(2)}, u32[]{:S(2)}) collective-permute-start(bf16[160,1152]{1,0:T(8,128)(2,1)S(1)} %pad_maximum_fusion.refs_0_), channel_id=1, source_target_pairs={{0,4},{1,5},{2,6},{3,7},{4,0},{5,1},{6,2},{7,3},{8,12},{9,13},{10,... | collective-permute-start | bytes 1105928 | tf_op jit(solution)/shard_map/ppermute | solution.py:268
  49.8 18.0 %collective-permute-start.8 = (bf16[160,1152]{1,0:T(8,128)(2,1)S(1)}, bf16[160,1152]{1,0:T(8,128)(2,1)S(1)}, u32[]{:S(2)}, u32[]{:S(2)}) collective-permute-start(bf16[160,1152]{1,0:T(8,128)(2,1)S(1)} %pad_maximum_fusion.1.refs_1_), channel_id=1, source_target_pairs={{0,6},{1,7},{2,0},{3,1},{4,2},{5,3},{6,4},{7,5},{8,14},{9,15},{10,... | collective-permute-start | bytes 1105928 | tf_op jit(solution)/shard_map/ppermute | solution.py:268
  50.9 19.1 %collective-permute-start.7 = (bf16[160,1152]{1,0:T(8,128)(2,1)S(1)}, bf16[160,1152]{1,0:T(8,128)(2,1)S(1)}, u32[]{:S(2)}, u32[]{:S(2)}) collective-permute-start(bf16[160,1152]{1,0:T(8,128)(2,1)S(1)} %pad_maximum_fusion.1.refs_1_), channel_id=1, source_target_pairs={{0,4},{1,5},{2,6},{3,7},{4,0},{5,1},{6,2},{7,3},{8,12},{9,13},{10,... | collective-permute-start | bytes 1105928 | tf_op jit(solution)/shard_map/ppermute | solution.py:268
  52.6 23.1 %collective-permute-start.6 = (bf16[160,1152]{1,0:T(8,128)(2,1)S(1)}, bf16[160,1152]{1,0:T(8,128)(2,1)S(1)}, u32[]{:S(2)}, u32[]{:S(2)}) collective-permute-start(bf16[160,1152]{1,0:T(8,128)(2,1)S(1)} %pad_maximum_fusion.1.refs_1_), channel_id=1, source_target_pairs={{0,2},{1,3},{2,4},{3,5},{4,6},{5,7},{6,0},{7,1},{8,10},{9,11},{10,... | collective-permute-start | bytes 1105928 | tf_op jit(solution)/shard_map/ppermute | solution.py:268
  67.8 2.2 %copy-start.11 = (bf16[160,1152]{1,0:T(8,128)(2,1)}, bf16[160,1152]{1,0:T(8,128)(2,1)S(1)}, u32[]{:S(2)}) copy-start(bf16[160,1152]{1,0:T(8,128)(2,1)S(1)} %collective-permute-done.8.refs_7_) | copy-start | bytes 1105924
  70.0 0.7 copy-start.12
  78.7 3.0 %collective-permute-start.9 = (bf16[16,40,864]{2,1,0:T(8,128)(2,1)}, bf16[16,40,864]{2,1,0:T(8,128)(2,1)S(1)}, u32[]{:S(2)}, u32[]{:S(2)}) collective-permute-start(bf16[16,40,864]{2,1,0:T(8,128)(2,1)} %all-to-all-done.1.refs_8_), channel_id=1, source_target_pairs={{0,1},{1,0},{2,3},{3,2},{4,5},{5,4},{6,7},{7,6},{8,9},{9,8},{10,11... | collective-permute-start | bytes 3317768 | tf_op jit(solution)/shard_map/ppermute | solution.py:272
  80.1 20.4 %collective-permute-start.11 = (bf16[288,1152]{1,0:T(8,128)(2,1)S(1)}, bf16[288,1152]{1,0:T(8,128)(2,1)S(1)}, u32[]{:S(2)}, u32[]{:S(2)}) collective-permute-start(bf16[288,1152]{1,0:T(8,128)(2,1)S(1)} %get-tuple-element.71), channel_id=1, source_target_pairs={{0,136},{1,137},{2,138},{3,139},{4,140},{5,141},{6,142},{7,143},{8... | collective-permute-start | bytes 1990664 | tf_op jit(solution)/shard_map/ppermute | solution.py:288
  81.8 18.8 %collective-permute-start.10 = (bf16[288,1152]{1,0:T(8,128)(2,1)S(1)}, bf16[288,1152]{1,0:T(8,128)(2,1)S(1)}, u32[]{:S(2)}, u32[]{:S(2)}) collective-permute-start(bf16[288,1152]{1,0:T(8,128)(2,1)S(1)} %get-tuple-element.72), channel_id=1, source_target_pairs={{0,128},{1,129},{2,130},{3,131},{4,132},{5,133},{6,134},{7,135},{8... | collective-permute-start | bytes 1990664 | tf_op jit(solution)/shard_map/ppermute | solution.py:288
  81.8 1.0 copy-start.6
  100.5 0.9 copy-start.7
  101.4 0.9 copy-start.9
  102.2 25.2 %collective-permute-start.12 = (bf16[576,1152]{1,0:T(8,128)(2,1)}, bf16[576,1152]{1,0:T(8,128)(2,1)S(1)}, u32[]{:S(2)}, u32[]{:S(2)}) collective-permute-start(bf16[576,1152]{1,0:T(8,128)(2,1)} %all-gather.3.cloned.1.call-done.m0), channel_id=1, source_target_pairs={{0,1},{1,0},{2,3},{3,2},{4,5},{5,4},{6,7},{7,6},{8,9},{9,8},{10,11... | collective-permute-start | bytes 3981320 | tf_op jit(solution)/shard_map/ppermute | solution.py:272
  102.5 6.9 %copy-start.8 = (bf16[288,1152]{1,0:T(8,128)(2,1)S(1)}, bf16[288,1152]{1,0:T(8,128)(2,1)}, u32[]{:S(2)}) copy-start(bf16[288,1152]{1,0:T(8,128)(2,1)} %copy-done.7) | copy-start | bytes 1990660
  102.5 23.8 %all-to-all-start.2 = ((bf16[16,80,288]{2,1,0:T(8,128)(2,1)}), bf16[16,80,288]{2,1,0:T(8,128)(2,1)S(1)}, u32[]{:S(2)}, u32[]{:S(2)}) async-start(bf16[16,80,288]{2,1,0:T(8,128)(2,1)} %shard_map.66), calls=%async_computation.2 | async-start | bytes 1966080 | tf_op jit(solution)/shard_map/all_to_all | solution.py:368
  109.0 18.4 %collective-permute-start.13 = (bf16[288,1152]{1,0:T(8,128)(2,1)}, bf16[288,1152]{1,0:T(8,128)(2,1)}, u32[]{:S(2)}, u32[]{:S(2)}) collective-permute-start(bf16[288,1152]{1,0:T(8,128)(2,1)} %copy-done.9), channel_id=1, source_target_pairs={{0,1},{1,0},{2,3},{3,2},{4,5},{5,4},{6,7},{7,6},{8,9},{9,8},{10,11... | collective-permute-start | bytes 1990664 | tf_op jit(solution)/shard_map/ppermute | solution.py:272
  109.4 18.0 %collective-permute-start.14 = (bf16[288,1152]{1,0:T(8,128)(2,1)S(1)}, bf16[288,1152]{1,0:T(8,128)(2,1)}, u32[]{:S(2)}, u32[]{:S(2)}) collective-permute-start(bf16[288,1152]{1,0:T(8,128)(2,1)S(1)} %copy-done.8), channel_id=1, source_target_pairs={{0,1},{1,0},{2,3},{3,2},{4,5},{5,4},{6,7},{7,6},{8,9},{9,8},{10,11... | collective-permute-start | bytes 1990664 | tf_op jit(solution)/shard_map/ppermute | solution.py:272
  126.2 1.1 copy-start.4
  126.2 36.1 %collective-permute-start.15 = (bf16[512,1152]{1,0:T(8,128)(2,1)}, bf16[512,1152]{1,0:T(8,128)(2,1)}, u32[]{:S(2)}, u32[]{:S(2)}) collective-permute-start(bf16[512,1152]{1,0:T(8,128)(2,1)} %get-tuple-element.66), channel_id=1, source_target_pairs={{0,128},{1,129},{2,130},{3,131},{4,132},{5,133},{6,134},{7,135},{8... | collective-permute-start | bytes 3538952 | tf_op jit(solution)/shard_map/ppermute | solution.py:288
  126.3 36.1 %collective-permute-start.16 = (bf16[512,1152]{1,0:T(8,128)(2,1)}, bf16[512,1152]{1,0:T(8,128)(2,1)}, u32[]{:S(2)}, u32[]{:S(2)}) collective-permute-start(bf16[512,1152]{1,0:T(8,128)(2,1)} %get-tuple-element.67), channel_id=1, source_target_pairs={{0,136},{1,137},{2,138},{3,139},{4,140},{5,141},{6,142},{7,143},{8... | collective-permute-start | bytes 3538952 | tf_op jit(solution)/shard_map/ppermute | solution.py:288
  127.4 1.1 copy-start.5
  128.5 7.0 %copy-start.1 = (bf16[1024,1152]{1,0:T(8,128)(2,1)S(1)}, bf16[1024,1152]{1,0:T(8,128)(2,1)}, u32[]{:S(2)}) copy-start(bf16[1024,1152]{1,0:T(8,128)(2,1)} %all-gather.5.cloned.1.call-done.refs_0_) | copy-start | bytes 7077892
  135.5 31.6 %collective-permute-start.17 = (bf16[1024,1152]{1,0:T(8,128)(2,1)S(1)}, bf16[1024,1152]{1,0:T(8,128)(2,1)}, u32[]{:S(2)}, u32[]{:S(2)}) collective-permute-start(bf16[1024,1152]{1,0:T(8,128)(2,1)S(1)} %copy-done.1), channel_id=1, source_target_pairs={{0,1},{1,0},{2,3},{3,2},{4,5},{5,4},{6,7},{7,6},{8,9},{9,8},{10,11... | collective-permute-start | bytes 7077896 | tf_op jit(solution)/shard_map/ppermute | solution.py:272
  135.6 28.5 %all-to-all-start.3 = ((bf16[16,24,1152]{2,1,0:T(8,128)(2,1)}), bf16[16,24,1152]{2,1,0:T(8,128)(2,1)}, u32[]{:S(2)}, u32[]{:S(2)}) async-start(bf16[16,24,1152]{2,1,0:T(8,128)(2,1)} %get-tuple-element.62), calls=%async_computation.3 | async-start | bytes 1769472 | tf_op jit(solution)/shard_map/all_to_all | solution.py:391
  162.3 3.2 %collective-permute-start.18 = (bf16[512,1152]{1,0:T(8,128)(2,1)}, bf16[512,1152]{1,0:T(8,128)(2,1)}, u32[]{:S(2)}, u32[]{:S(2)}) collective-permute-start(bf16[512,1152]{1,0:T(8,128)(2,1)} %collective-permute-done.15.refs_1_), channel_id=1, source_target_pairs={{0,1},{1,0},{2,3},{3,2},{4,5},{5,4},{6,7},{7,6},{8,9},{9,8},{10,11... | collective-permute-start | bytes 3538952 | tf_op jit(solution)/shard_map/ppermute | solution.py:272
  162.3 4.9 %collective-permute-start.19 = (bf16[512,1152]{1,0:T(8,128)(2,1)}, bf16[512,1152]{1,0:T(8,128)(2,1)}, u32[]{:S(2)}, u32[]{:S(2)}) collective-permute-start(bf16[512,1152]{1,0:T(8,128)(2,1)} %collective-permute-done.16.refs_2_), channel_id=1, source_target_pairs={{0,1},{1,0},{2,3},{3,2},{4,5},{5,4},{6,7},{7,6},{8,9},{9,8},{10,11... | collective-permute-start | bytes 3538952 | tf_op jit(solution)/shard_map/ppermute | solution.py:272
Sparse Core Ops, SparseCore 0:
  15.6 52.7 all-gather.2
  70.3 40.2 all-gather.4
where the time goes:
time: 223 us; the launch traced here: 222 us
  waiting for transfers between devices  75.2 us (34%)
  Pallas kernels  47.9 us (21%)
  starting transfers between devices  43.5 us (20%)
  blocking collectives  28.7 us (13%)
  between operations  13.6 us (6%)
  local copies, waits for them, and re-layouts  13.2 us (6%)
    all_to_all x1, blocking collectives, on_device(): o_t = lax.all_to_all(o_t, 'frame', 0, 0, tiled=True)  28.7 us
    ppermute x4, waiting for transfers between devices, from_y_neighbours(): got.append(lax.ppermute(part, ('frame', 'row'), pairs))  21.9 us
    ppermute x6, waiting for transfers between devices, shift_x(): return lax.ppermute(value, 'row', pairs)  21 us
    pallas_call x1, Pallas kernels, on_device(): call(spatial_kernel, sds((16, tokens, GROUP)), 10, scratch=[pltpu.VMEM((1...  17.7 us
    pallas_call x1, Pallas kernels, on_device(): call(temporal_kernel, sds((16, 24, D)), 7, scratch=[pltpu.VMEM((2, 2, 320...  14 us
    all_to_all x1, waiting for transfers between devices, on_device(): o_s = lax.all_to_all(o_s, 'row', 0, 0, tiled=True)  12.5 us
    all_to_all x1, waiting for transfers between devices, on_device(): lax.all_to_all(first.reshape(16, 36, 216), 'frame', 0, 0, tiled=True)  10.8 us
    all_to_all x1, starting transfers between devices, on_device(): lax.all_to_all(first.reshape(16, 36, 216), 'frame', 0, 0, tiled=True)  8.7 us
  transfers between devices with their start and end apart: 26, of which 12 were waited for; matrix products, arithmetic and copies ran while one was open for 3% of the time, Pallas kernels for 13%

commit v1 on v0

--- a/solution.py
+++ b/solution.py
@@ -366,7 +366,8 @@
     o_s, *proj = lax.optimization_barrier((o_s, *proj))
     proj_other = [swap_core(v) for v in proj]
     o_s = lax.all_to_all(o_s, "row", 0, 0, tiled=True)
-    _, tq, *parts = lax.optimization_barrier((o_s, tq, *halves(tq)))
+    near_out, tq, *parts = lax.optimization_barrier((proj_other[0], tq, *halves(tq)))
+    proj_other[0] = near_out
     tq = [tq] + from_y_neighbours(parts)
 
     mid, chunks = call(

time: 223 us -> 219 us (0.982)
  waiting for transfers between devices: 75.2 us -> 69 us
    all_to_all x1, waiting for transfers between devices: 1.29 us -> 13.1 us  [on_device(): chunks = lax.all_to_all(chunks, 'frame', 0, 0, tiled=True)]
    ppermute x4, waiting for transfers between devices: 21.9 us -> 10.6 us  [from_y_neighbours(): got.append(lax.ppermute(part, ('frame', 'row'), pairs))]
    all_to_all x1, waiting for transfers between devices: 12.5 us -> 8.91 us  [on_device(): o_s = lax.all_to_all(o_s, 'row', 0, 0, tiled=True)]
    ppermute x9, waiting for transfers between devices: 3.08 us -> 0.02 us  [swap_core(): return lax.ppermute(value, 'row', [(r, r ^ 1) for r in range(16)])]
    ppermute x4, starting transfers between devices: 2.77 us -> 5.28 us  [from_y_neighbours(): got.append(lax.ppermute(part, ('frame', 'row'), pairs))]
  transfers between devices with their start and end apart: 26 -> 26, of which waited for: 12 -> 11; matrix products, arithmetic and copies ran while one was open for 3% -> 3% of each run, Pallas kernels for 13% -> 13%
where the time goes in v1:
time: 219 us; the launch traced here: 218 us
  waiting for transfers between devices  69 us (32%)
  Pallas kernels  47.9 us (22%)
  starting transfers between devices  45.3 us (21%)
  blocking collectives  28.9 us (13%)
  between operations  13.6 us (6%)
  local copies, waits for them, and re-layouts  13.1 us (6%)
    all_to_all x1, blocking collectives, on_device(): o_t = lax.all_to_all(o_t, 'frame', 0, 0, tiled=True)  28.9 us
    ppermute x6, waiting for transfers between devices, shift_x(): return lax.ppermute(value, 'row', pairs)  21 us
    pallas_call x1, Pallas kernels, on_device(): call(spatial_kernel, sds((16, tokens, GROUP)), 10, scratch=[pltpu.VMEM((1...  17.7 us
    pallas_call x1, Pallas kernels, on_device(): call(temporal_kernel, sds((16, 24, D)), 7, scratch=[pltpu.VMEM((2, 2, 320...  14 us
    all_to_all x1, waiting for transfers between devices, on_device(): chunks = lax.all_to_all(chunks, 'frame', 0, 0, tiled=True)  13.1 us
    all_to_all x1, waiting for transfers between devices, on_device(): lax.all_to_all(first.reshape(16, 36, 216), 'frame', 0, 0, tiled=True)  10.8 us
    ppermute x4, waiting for transfers between devices, from_y_neighbours(): got.append(lax.ppermute(part, ('frame', 'row'), pairs))  10.6 us
    all_to_all x1, waiting for transfers between devices, on_device(): o_s = lax.all_to_all(o_s, 'row', 0, 0, tiled=True)  8.91 us
  transfers between devices with their start and end apart: 26, of which 11 were waited for; matrix products, arithmetic and copies ran while one was open for 3% of the time, Pallas kernels for 13%

profile of v1, /device:TPU:32, one launch (start us, length us, event | category | flops | bytes accessed | tf_op | source)
XLA Modules:
  0.0 217.9 jit_solution(10172029152120038673)
XLA Ops:
  6.5 1.0 copy-done
  7.6 0.2 constant_dynamic-slice_fusion
  7.7 0.0 copy-start.2
  7.7 1.1 copy-done.2
  8.8 0.8 copy-done.3
  9.6 0.5 shard_map.64
  10.2 0.1 collective-permute-start
  10.3 3.3 %collective-permute-start.3 = (bf16[2,80,1152]{2,1,0:T(8,128)(2,1)S(1)}, bf16[2,80,1152]{2,1,0:T(8,128)(2,1)S(1)}, u32[]{:S(2)}, u32[]{:S(2)}) collective-permute-start(bf16[2,80,1152]{2,1,0:T(8,128)(2,1)S(1)} %get-tuple-element.45), channel_id=1, source_target_pairs={{0,8},{1,9},{2,10},{3,11},{4,12},{5,13},{6,14},{7,15},{8,0},{9,1},... | collective-permute-start | bytes 1105928 | tf_op jit(solution)/shard_map/ppermute | solution.py:276
  13.5 2.0 shard_map.67
  15.5 0.0 all-gather.3.cloned.1.call-update
  15.5 0.0 collective-permute-done
  15.6 0.2 copy.8
  15.7 0.8 reshape.10
  16.5 8.7 %all-to-all-start = ((bf16[16,36,216]{2,1,0:T(8,128)(2,1)}), bf16[16,36,216]{2,1,0:T(8,128)(2,1)S(1)}, u32[]{:S(2)}, u32[]{:S(2)}) async-start(bf16[16,36,216]{2,1,0:T(8,128)(2,1)} %reshape.10), calls=%async_computation | async-start | bytes 655360 | tf_op jit(solution)/shard_map/all_to_all | solution.py:330
  25.2 0.0 collective-permute-done.3
  25.3 0.1 collective-permute-start.4
  25.4 2.8 %collective-permute-start.2 = (bf16[160,1152]{1,0:T(8,128)(2,1)S(1)}, bf16[160,1152]{1,0:T(8,128)(2,1)S(1)}, u32[]{:S(2)}, u32[]{:S(2)}) collective-permute-start(bf16[160,1152]{1,0:T(8,128)(2,1)S(1)} %pad_maximum_fusion.refs_0_), channel_id=1, source_target_pairs={{0,6},{1,7},{2,0},{3,1},{4,2},{5,3},{6,4},{7,5},{8,14},{9,15},{10,... | collective-permute-start | bytes 1105928 | tf_op jit(solution)/shard_map/ppermute | solution.py:268
  28.3 10.8 %all-to-all-done.w_ref = bf16[16,36,216]{2,1,0:T(8,128)(2,1)S(1)} async-done(((bf16[16,36,216]{2,1,0:T(8,128)(2,1)}), bf16[16,36,216]{2,1,0:T(8,128)(2,1)S(1)}, u32[]{:S(2)}, u32[]{:S(2)}) %all-to-all-start) | async-done | bytes 248864 | tf_op jit(solution)/shard_map/all_to_all | solution.py:330
  39.0 1.2 shard_map.65
  40.2 0.0 collective-permute-done.2.refs_6_
  40.2 0.0 collective-permute-done.1.refs_2_
  40.2 8.0 %all-to-all-start.1 = ((bf16[16,40,864]{2,1,0:T(8,128)(2,1)}), bf16[16,40,864]{2,1,0:T(8,128)(2,1)}, u32[]{:S(2)}, u32[]{:S(2)}) async-start(bf16[16,40,864]{2,1,0:T(8,128)(2,1)} %shard_map.65), calls=%async_computation.1 | async-start | bytes 2293760 | tf_op jit(solution)/shard_map/all_to_all | solution.py:340
  48.2 0.0 all-gather.5.cloned.1.call-start
  48.3 0.7 all-gather.5.cloned.1.call-update
  49.0 0.8 collective-permute-start.5
  49.8 1.1 collective-permute-start.8
  50.9 1.7 collective-permute-start.7
  52.6 1.4 collective-permute-start.6
  54.0 8.2 %collective-permute-done.5.refs_4_ = bf16[160,1152]{1,0:T(8,128)(2,1)S(1)} collective-permute-done((bf16[160,1152]{1,0:T(8,128)(2,1)S(1)}, bf16[160,1152]{1,0:T(8,128)(2,1)S(1)}, u32[]{:S(2)}, u32[]{:S(2)}) %collective-permute-start.5) | collective-permute-done | bytes 368672 | tf_op jit(solution)/shard_map/ppermute | solution.py:268
  62.2 5.6 %collective-permute-done.8.refs_7_ = bf16[160,1152]{1,0:T(8,128)(2,1)S(1)} collective-permute-done((bf16[160,1152]{1,0:T(8,128)(2,1)S(1)}, bf16[160,1152]{1,0:T(8,128)(2,1)S(1)}, u32[]{:S(2)}, u32[]{:S(2)}) %collective-permute-start.8) | collective-permute-done | bytes 368672 | tf_op jit(solution)/shard_map/ppermute | solution.py:268
  67.8 2.2 %collective-permute-done.7.refs_5_ = bf16[160,1152]{1,0:T(8,128)(2,1)S(1)} collective-permute-done((bf16[160,1152]{1,0:T(8,128)(2,1)S(1)}, bf16[160,1152]{1,0:T(8,128)(2,1)S(1)}, u32[]{:S(2)}, u32[]{:S(2)}) %collective-permute-start.7) | collective-permute-done | bytes 368672 | tf_op jit(solution)/shard_map/ppermute | solution.py:268
  70.0 0.7 copy-done.12
  70.8 5.0 %collective-permute-done.6.refs_3_ = bf16[160,1152]{1,0:T(8,128)(2,1)S(1)} collective-permute-done((bf16[160,1152]{1,0:T(8,128)(2,1)S(1)}, bf16[160,1152]{1,0:T(8,128)(2,1)S(1)}, u32[]{:S(2)}, u32[]{:S(2)}) %collective-permute-start.6) | collective-permute-done | bytes 368672 | tf_op jit(solution)/shard_map/ppermute | solution.py:268
  75.7 3.0 %all-to-all-done.1.refs_8_ = bf16[16,40,864]{2,1,0:T(8,128)(2,1)} async-done(((bf16[16,40,864]{2,1,0:T(8,128)(2,1)}), bf16[16,40,864]{2,1,0:T(8,128)(2,1)}, u32[]{:S(2)}, u32[]{:S(2)}) %all-to-all-start.1) | async-done | bytes 1105952 | tf_op jit(solution)/shard_map/all_to_all | solution.py:340
  78.7 0.0 collective-permute-start.9
  78.7 1.4 fusion.1
  80.1 1.6 collective-permute-start.11
  81.8 0.0 collective-permute-start.10
  81.8 1.0 copy-done.6
  82.8 17.7 %shard_map.66 = bf16[16,80,288]{2,1,0:T(8,128)(2,1)} custom-call(bf16[160,1152]{1,0:T(8,128)(2,1)S(1)} %pad_maximum_fusion.refs_0_, bf16[160,1152]{1,0:T(8,128)(2,1)S(1)} %pad_maximum_fusion.1.refs_1_, bf16[160,1152]{1,0:T(8,128)(2,1)S(1)} %collective-permute-done.1.refs_2_, bf16[160,1152]{1,0:T(8,128)(2,1)S(1)} %collective-permute-done.6.refs_3_, ...), custom_call_target="tpu_custom_call" | custom-call | flops 15000000512 | bytes 15000000 | tf_op jit(solution)/shard_map/pallas_call | solution.py:346
  100.5 0.8 copy-done.7
  101.4 0.9 copy-done.9
  102.2 0.2 collective-permute-start.12
  102.5 6.5 %all-to-all-start.2 = ((bf16[16,80,288]{2,1,0:T(8,128)(2,1)}), bf16[16,80,288]{2,1,0:T(8,128)(2,1)S(1)}, u32[]{:S(2)}, u32[]{:S(2)}) async-start(bf16[16,80,288]{2,1,0:T(8,128)(2,1)} %shard_map.66), calls=%async_computation.2 | async-start | bytes 1966080 | tf_op jit(solution)/shard_map/all_to_all | solution.py:368
  109.0 0.4 collective-permute-start.13
  109.4 0.2 collective-permute-start.14
  109.6 1.0 all-gather.5.cloned.1.call-done.refs_0_
  110.6 3.2 %fusion = (bf16[512,1152]{1,0:T(8,128)(2,1)}, bf16[512,1152]{1,0:T(8,128)(2,1)}) fusion(bf16[1024,1152]{1,0:T(8,128)(2,1)} %all-gather.5.cloned.1.call-done.refs_0_), kind=kLoop, calls=%fused_computation.5 | loop fusion | bytes 4718592 | tf_op jit(solution)/shard_map/slice | solution.py:281
  113.8 0.0 collective-permute-done.12.n0
  113.8 1.6 collective-permute-start.15
  115.4 2.1 collective-permute-start.16
  117.4 8.9 %all-to-all-done.2.o_in = bf16[16,80,288]{2,1,0:T(8,128)(2,1)S(1)} async-done(((bf16[16,80,288]{2,1,0:T(8,128)(2,1)}), bf16[16,80,288]{2,1,0:T(8,128)(2,1)S(1)}, u32[]{:S(2)}, u32[]{:S(2)}) %all-to-all-start.2) | async-done | bytes 737312 | tf_op jit(solution)/shard_map/all_to_all | solution.py:368
  126.3 1.0 copy-done.4
  127.3 7.0 %shard_map.68 = (f32[320,1152]{1,0:T(8,128)}, bf16[16,24,1152]{2,1,0:T(8,128)(2,1)}) custom-call(bf16[16,80,288]{2,1,0:T(8,128)(2,1)} %copy-done.4, bf16[320,1152]{1,0:T(8,128)(2,1)} %bitcast.10, f32[6,1152]{1,0:T(8,128)} %mod_ref.5, bf16[576,1152]{1,0:T(8,128)(2,1)} %all-gather.3.cloned.1.call-done.m0, bf16[288,1152]{1,0:T(8,128)(2,1)} %copy-done.9, ...), custom_call_target="tpu_custom_call" | custom-call | flops 4000000000 | bytes 4000000 | tf_op jit(solution)/shard_map/pallas_call | solution.py:373
  134.3 0.1 collective-permute-start.17
  134.4 4.5 %all-to-all-start.3 = ((bf16[16,24,1152]{2,1,0:T(8,128)(2,1)}), bf16[16,24,1152]{2,1,0:T(8,128)(2,1)}, u32[]{:S(2)}, u32[]{:S(2)}) async-start(bf16[16,24,1152]{2,1,0:T(8,128)(2,1)} %get-tuple-element.65), calls=%async_computation.3 | async-start | bytes 1769472 | tf_op jit(solution)/shard_map/all_to_all | solution.py:392
  138.9 9.9 %collective-permute-done.15.refs_1_ = bf16[512,1152]{1,0:T(8,128)(2,1)} collective-permute-done((bf16[512,1152]{1,0:T(8,128)(2,1)}, bf16[512,1152]{1,0:T(8,128)(2,1)}, u32[]{:S(2)}, u32[]{:S(2)}) %collective-permute-start.15) | collective-permute-done | bytes 1179680 | tf_op jit(solution)/shard_map/ppermute | solution.py:288
  148.9 0.0 collective-permute-start.18
  148.9 0.7 collective-permute-done.16.refs_2_
  149.5 0.0 collective-permute-start.19
  149.5 13.1 %all-to-all-done.3.x_ref = bf16[16,24,1152]{2,1,0:T(8,128)(2,1)} async-done(((bf16[16,24,1152]{2,1,0:T(8,128)(2,1)}), bf16[16,24,1152]{2,1,0:T(8,128)(2,1)}, u32[]{:S(2)}, u32[]{:S(2)}) %all-to-all-start.3) | async-done | bytes 884768 | tf_op jit(solution)/shard_map/all_to_all | solution.py:392
  162.6 14.0 %shard_map.69 = bf16[16,24,1152]{2,1,0:T(8,128)(2,1)S(1)} custom-call(bf16[16,24,1152]{2,1,0:T(8,128)(2,1)} %all-to-all-done.3.x_ref, bf16[1024,1152]{1,0:T(8,128)(2,1)S(1)} %copy-done.1, bf16[512,1152]{1,0:T(8,128)(2,1)} %collective-permute-done.15.refs_1_, bf16[512,1152]{1,0:T(8,128)(2,1)} %collective-permute-done.16.refs_2_, ...), custom_call_target="tpu_custom_call" | custom-call | flops 12000000000 | bytes 12000000 | tf_op jit(solution)/shard_map/pallas_call | solution.py:394
  176.6 28.9 %all_to_all.25.o_in = bf16[16,24,1152]{2,1,0:T(8,128)(2,1)} all-to-all(bf16[16,24,1152]{2,1,0:T(8,128)(2,1)S(1)} %shard_map.69), channel_id=1, replica_groups=mesh['frame'=16,'row'=16] {'frame'}, dimensions={0} | all-to-all | bytes 1769472 | tf_op jit(solution)/shard_map/all_to_all | solution.py:402
  205.5 5.5 %shard_map.70 = bf16[320,1152]{1,0:T(8,128)(2,1)} custom-call(bf16[16,24,1152]{2,1,0:T(8,128)(2,1)} %all_to_all.25.o_in, f32[320,1152]{1,0:T(8,128)} %get-tuple-element.70.mid_in, f32[6,1152]{1,0:T(8,128)} %mod_ref.5, bf16[576,1152]{1,0:T(8,128)(2,1)} %all-gather.3.cloned.1.call-done.m0, bf16[288,1152]{1,0:T(8,128)(2,1)} %copy-done.9, ...), custom_call_target="tpu_custom_call" | custom-call | flops 4000000000 | bytes 4000000 | tf_op jit(solution)/shard_map/pallas_call | solution.py:403
  (32 shorter events, 0.2 us)
Async XLA Ops:
  6.5 1.0 copy-start
  6.5 72.2 %all-gather.3.cloned.1.call-start = ((), (), s32[]{:S(2)}) async-start(), calls=%async_computation.5 | async-start | bytes 1492992 | tf_op jit(solution)/shard_map/all_gather | solution.py:294
  7.7 1.1 copy-start.2
  8.8 0.8 copy-start.3
  10.2 5.4 %collective-permute-start = (bf16[80,1152]{1,0:T(8,128)(2,1)S(1)}, bf16[80,1152]{1,0:T(8,128)(2,1)S(1)}, u32[]{:S(2)}, u32[]{:S(2)}) collective-permute-start(bf16[80,1152]{1,0:T(8,128)(2,1)S(1)} %get-tuple-element.42), channel_id=1, source_target_pairs={{0,1},{1,0},{2,3},{3,2},{4,5},{5,4},{6,7},{7,6},{8,9},{9,8},{10,11... | collective-permute-start | bytes 552968 | tf_op jit(solution)/shard_map/ppermute | solution.py:272
  10.3 15.0 %collective-permute-start.3 = (bf16[2,80,1152]{2,1,0:T(8,128)(2,1)S(1)}, bf16[2,80,1152]{2,1,0:T(8,128)(2,1)S(1)}, u32[]{:S(2)}, u32[]{:S(2)}) collective-permute-start(bf16[2,80,1152]{2,1,0:T(8,128)(2,1)S(1)} %get-tuple-element.45), channel_id=1, source_target_pairs={{0,8},{1,9},{2,10},{3,11},{4,12},{5,13},{6,14},{7,15},{8,0},{9,1},... | collective-permute-start | bytes 1105928 | tf_op jit(solution)/shard_map/ppermute | solution.py:276
  16.5 22.5 %all-to-all-start = ((bf16[16,36,216]{2,1,0:T(8,128)(2,1)}), bf16[16,36,216]{2,1,0:T(8,128)(2,1)S(1)}, u32[]{:S(2)}, u32[]{:S(2)}) async-start(bf16[16,36,216]{2,1,0:T(8,128)(2,1)} %reshape.10), calls=%async_computation | async-start | bytes 655360 | tf_op jit(solution)/shard_map/all_to_all | solution.py:330
  25.3 2.9 %collective-permute-start.4 = (bf16[80,1152]{1,0:T(8,128)(2,1)S(1)}, bf16[80,1152]{1,0:T(8,128)(2,1)S(1)}, u32[]{:S(2)}, u32[]{:S(2)}) collective-permute-start(bf16[80,1152]{1,0:T(8,128)(2,1)S(1)} %get-tuple-element.76), channel_id=1, source_target_pairs={{0,1},{1,0},{2,3},{3,2},{4,5},{5,4},{6,7},{7,6},{8,9},{9,8},{10,11... | collective-permute-start | bytes 552968 | tf_op jit(solution)/shard_map/ppermute | solution.py:272
  25.4 14.8 %collective-permute-start.2 = (bf16[160,1152]{1,0:T(8,128)(2,1)S(1)}, bf16[160,1152]{1,0:T(8,128)(2,1)S(1)}, u32[]{:S(2)}, u32[]{:S(2)}) collective-permute-start(bf16[160,1152]{1,0:T(8,128)(2,1)S(1)} %pad_maximum_fusion.refs_0_), channel_id=1, source_target_pairs={{0,6},{1,7},{2,0},{3,1},{4,2},{5,3},{6,4},{7,5},{8,14},{9,15},{10,... | collective-permute-start | bytes 1105928 | tf_op jit(solution)/shard_map/ppermute | solution.py:268
  28.2 12.0 %collective-permute-start.1 = (bf16[160,1152]{1,0:T(8,128)(2,1)S(1)}, bf16[160,1152]{1,0:T(8,128)(2,1)S(1)}, u32[]{:S(2)}, u32[]{:S(2)}) collective-permute-start(bf16[160,1152]{1,0:T(8,128)(2,1)S(1)} %pad_maximum_fusion.refs_0_), channel_id=1, source_target_pairs={{0,2},{1,3},{2,4},{3,5},{4,6},{5,7},{6,0},{7,1},{8,10},{9,11},{10,... | collective-permute-start | bytes 1105928 | tf_op jit(solution)/shard_map/ppermute | solution.py:268
  40.2 8.7 %copy-start.10 = (bf16[160,1152]{1,0:T(8,128)(2,1)}, bf16[160,1152]{1,0:T(8,128)(2,1)S(1)}, u32[]{:S(2)}) copy-start(bf16[160,1152]{1,0:T(8,128)(2,1)S(1)} %collective-permute-done.2.refs_6_) | copy-start | bytes 1105924
  40.2 38.5 %all-to-all-start.1 = ((bf16[16,40,864]{2,1,0:T(8,128)(2,1)}), bf16[16,40,864]{2,1,0:T(8,128)(2,1)}, u32[]{:S(2)}, u32[]{:S(2)}) async-start(bf16[16,40,864]{2,1,0:T(8,128)(2,1)} %shard_map.65), calls=%async_computation.1 | async-start | bytes 2293760 | tf_op jit(solution)/shard_map/all_to_all | solution.py:340
  48.2 62.3 %all-gather.5.cloned.1.call-start = ((), (), s32[]{:S(2)}) async-start(), calls=%async_computation.6 | async-start | bytes 2654208 | tf_op jit(solution)/shard_map/all_gather | solution.py:294
  49.0 13.2 %collective-permute-start.5 = (bf16[160,1152]{1,0:T(8,128)(2,1)S(1)}, bf16[160,1152]{1,0:T(8,128)(2,1)S(1)}, u32[]{:S(2)}, u32[]{:S(2)}) collective-permute-start(bf16[160,1152]{1,0:T(8,128)(2,1)S(1)} %pad_maximum_fusion.refs_0_), channel_id=1, source_target_pairs={{0,4},{1,5},{2,6},{3,7},{4,0},{5,1},{6,2},{7,3},{8,12},{9,13},{10,... | collective-permute-start | bytes 1105928 | tf_op jit(solution)/shard_map/ppermute | solution.py:268
  49.8 18.0 %collective-permute-start.8 = (bf16[160,1152]{1,0:T(8,128)(2,1)S(1)}, bf16[160,1152]{1,0:T(8,128)(2,1)S(1)}, u32[]{:S(2)}, u32[]{:S(2)}) collective-permute-start(bf16[160,1152]{1,0:T(8,128)(2,1)S(1)} %pad_maximum_fusion.1.refs_1_), channel_id=1, source_target_pairs={{0,6},{1,7},{2,0},{3,1},{4,2},{5,3},{6,4},{7,5},{8,14},{9,15},{10,... | collective-permute-start | bytes 1105928 | tf_op jit(solution)/shard_map/ppermute | solution.py:268
  50.9 19.1 %collective-permute-start.7 = (bf16[160,1152]{1,0:T(8,128)(2,1)S(1)}, bf16[160,1152]{1,0:T(8,128)(2,1)S(1)}, u32[]{:S(2)}, u32[]{:S(2)}) collective-permute-start(bf16[160,1152]{1,0:T(8,128)(2,1)S(1)} %pad_maximum_fusion.1.refs_1_), channel_id=1, source_target_pairs={{0,4},{1,5},{2,6},{3,7},{4,0},{5,1},{6,2},{7,3},{8,12},{9,13},{10,... | collective-permute-start | bytes 1105928 | tf_op jit(solution)/shard_map/ppermute | solution.py:268
  52.6 23.1 %collective-permute-start.6 = (bf16[160,1152]{1,0:T(8,128)(2,1)S(1)}, bf16[160,1152]{1,0:T(8,128)(2,1)S(1)}, u32[]{:S(2)}, u32[]{:S(2)}) collective-permute-start(bf16[160,1152]{1,0:T(8,128)(2,1)S(1)} %pad_maximum_fusion.1.refs_1_), channel_id=1, source_target_pairs={{0,2},{1,3},{2,4},{3,5},{4,6},{5,7},{6,0},{7,1},{8,10},{9,11},{10,... | collective-permute-start | bytes 1105928 | tf_op jit(solution)/shard_map/ppermute | solution.py:268
  67.8 2.2 %copy-start.11 = (bf16[160,1152]{1,0:T(8,128)(2,1)}, bf16[160,1152]{1,0:T(8,128)(2,1)S(1)}, u32[]{:S(2)}) copy-start(bf16[160,1152]{1,0:T(8,128)(2,1)S(1)} %collective-permute-done.8.refs_7_) | copy-start | bytes 1105924
  70.0 0.7 copy-start.12
  78.7 3.0 %collective-permute-start.9 = (bf16[16,40,864]{2,1,0:T(8,128)(2,1)}, bf16[16,40,864]{2,1,0:T(8,128)(2,1)S(1)}, u32[]{:S(2)}, u32[]{:S(2)}) collective-permute-start(bf16[16,40,864]{2,1,0:T(8,128)(2,1)} %all-to-all-done.1.refs_8_), channel_id=1, source_target_pairs={{0,1},{1,0},{2,3},{3,2},{4,5},{5,4},{6,7},{7,6},{8,9},{9,8},{10,11... | collective-permute-start | bytes 3317768 | tf_op jit(solution)/shard_map/ppermute | solution.py:272
  80.1 20.4 %collective-permute-start.11 = (bf16[288,1152]{1,0:T(8,128)(2,1)S(1)}, bf16[288,1152]{1,0:T(8,128)(2,1)S(1)}, u32[]{:S(2)}, u32[]{:S(2)}) collective-permute-start(bf16[288,1152]{1,0:T(8,128)(2,1)S(1)} %get-tuple-element.73), channel_id=1, source_target_pairs={{0,136},{1,137},{2,138},{3,139},{4,140},{5,141},{6,142},{7,143},{8... | collective-permute-start | bytes 1990664 | tf_op jit(solution)/shard_map/ppermute | solution.py:288
  81.8 18.8 %collective-permute-start.10 = (bf16[288,1152]{1,0:T(8,128)(2,1)S(1)}, bf16[288,1152]{1,0:T(8,128)(2,1)S(1)}, u32[]{:S(2)}, u32[]{:S(2)}) collective-permute-start(bf16[288,1152]{1,0:T(8,128)(2,1)S(1)} %get-tuple-element.74), channel_id=1, source_target_pairs={{0,128},{1,129},{2,130},{3,131},{4,132},{5,133},{6,134},{7,135},{8... | collective-permute-start | bytes 1990664 | tf_op jit(solution)/shard_map/ppermute | solution.py:288
  81.8 1.0 copy-start.6
  100.5 0.9 copy-start.7
  101.4 0.9 copy-start.9
  102.2 11.5 %collective-permute-start.12 = (bf16[576,1152]{1,0:T(8,128)(2,1)}, bf16[576,1152]{1,0:T(8,128)(2,1)S(1)}, u32[]{:S(2)}, u32[]{:S(2)}) collective-permute-start(bf16[576,1152]{1,0:T(8,128)(2,1)} %all-gather.3.cloned.1.call-done.m0), channel_id=1, source_target_pairs={{0,1},{1,0},{2,3},{3,2},{4,5},{5,4},{6,7},{7,6},{8,9},{9,8},{10,11... | collective-permute-start | bytes 3981320 | tf_op jit(solution)/shard_map/ppermute | solution.py:272
  102.5 6.9 %copy-start.8 = (bf16[288,1152]{1,0:T(8,128)(2,1)S(1)}, bf16[288,1152]{1,0:T(8,128)(2,1)}, u32[]{:S(2)}) copy-start(bf16[288,1152]{1,0:T(8,128)(2,1)} %copy-done.7) | copy-start | bytes 1990660
  102.5 23.9 %all-to-all-start.2 = ((bf16[16,80,288]{2,1,0:T(8,128)(2,1)}), bf16[16,80,288]{2,1,0:T(8,128)(2,1)S(1)}, u32[]{:S(2)}, u32[]{:S(2)}) async-start(bf16[16,80,288]{2,1,0:T(8,128)(2,1)} %shard_map.66), calls=%async_computation.2 | async-start | bytes 1966080 | tf_op jit(solution)/shard_map/all_to_all | solution.py:368
  109.0 8.4 %collective-permute-start.13 = (bf16[288,1152]{1,0:T(8,128)(2,1)}, bf16[288,1152]{1,0:T(8,128)(2,1)}, u32[]{:S(2)}, u32[]{:S(2)}) collective-permute-start(bf16[288,1152]{1,0:T(8,128)(2,1)} %copy-done.9), channel_id=1, source_target_pairs={{0,1},{1,0},{2,3},{3,2},{4,5},{5,4},{6,7},{7,6},{8,9},{9,8},{10,11... | collective-permute-start | bytes 1990664 | tf_op jit(solution)/shard_map/ppermute | solution.py:272
  109.4 8.0 %collective-permute-start.14 = (bf16[288,1152]{1,0:T(8,128)(2,1)S(1)}, bf16[288,1152]{1,0:T(8,128)(2,1)}, u32[]{:S(2)}, u32[]{:S(2)}) collective-permute-start(bf16[288,1152]{1,0:T(8,128)(2,1)S(1)} %copy-done.8), channel_id=1, source_target_pairs={{0,1},{1,0},{2,3},{3,2},{4,5},{5,4},{6,7},{7,6},{8,9},{9,8},{10,11... | collective-permute-start | bytes 1990664 | tf_op jit(solution)/shard_map/ppermute | solution.py:272
  113.8 12.6 %copy-start.5 = (bf16[576,1152]{1,0:T(8,128)(2,1)}, bf16[576,1152]{1,0:T(8,128)(2,1)S(1)}, u32[]{:S(2)}) copy-start(bf16[576,1152]{1,0:T(8,128)(2,1)S(1)} %collective-permute-done.12.n0) | copy-start | bytes 3981316
  113.8 35.1 %collective-permute-start.15 = (bf16[512,1152]{1,0:T(8,128)(2,1)}, bf16[512,1152]{1,0:T(8,128)(2,1)}, u32[]{:S(2)}, u32[]{:S(2)}) collective-permute-start(bf16[512,1152]{1,0:T(8,128)(2,1)} %get-tuple-element.68), channel_id=1, source_target_pairs={{0,128},{1,129},{2,130},{3,131},{4,132},{5,133},{6,134},{7,135},{8... | collective-permute-start | bytes 3538952 | tf_op jit(solution)/shard_map/ppermute | solution.py:288
  115.4 34.2 %collective-permute-start.16 = (bf16[512,1152]{1,0:T(8,128)(2,1)}, bf16[512,1152]{1,0:T(8,128)(2,1)}, u32[]{:S(2)}, u32[]{:S(2)}) collective-permute-start(bf16[512,1152]{1,0:T(8,128)(2,1)} %get-tuple-element.69), channel_id=1, source_target_pairs={{0,136},{1,137},{2,138},{3,139},{4,140},{5,141},{6,142},{7,143},{8... | collective-permute-start | bytes 3538952 | tf_op jit(solution)/shard_map/ppermute | solution.py:288
  126.3 1.0 copy-start.4
  127.3 7.0 %copy-start.1 = (bf16[1024,1152]{1,0:T(8,128)(2,1)S(1)}, bf16[1024,1152]{1,0:T(8,128)(2,1)}, u32[]{:S(2)}) copy-start(bf16[1024,1152]{1,0:T(8,128)(2,1)} %all-gather.5.cloned.1.call-done.refs_0_) | copy-start | bytes 7077892
  134.3 28.3 %collective-permute-start.17 = (bf16[1024,1152]{1,0:T(8,128)(2,1)S(1)}, bf16[1024,1152]{1,0:T(8,128)(2,1)}, u32[]{:S(2)}, u32[]{:S(2)}) collective-permute-start(bf16[1024,1152]{1,0:T(8,128)(2,1)S(1)} %copy-done.1), channel_id=1, source_target_pairs={{0,1},{1,0},{2,3},{3,2},{4,5},{5,4},{6,7},{7,6},{8,9},{9,8},{10,11... | collective-permute-start | bytes 7077896 | tf_op jit(solution)/shard_map/ppermute | solution.py:272
  134.4 28.2 %all-to-all-start.3 = ((bf16[16,24,1152]{2,1,0:T(8,128)(2,1)}), bf16[16,24,1152]{2,1,0:T(8,128)(2,1)}, u32[]{:S(2)}, u32[]{:S(2)}) async-start(bf16[16,24,1152]{2,1,0:T(8,128)(2,1)} %get-tuple-element.65), calls=%async_computation.3 | async-start | bytes 1769472 | tf_op jit(solution)/shard_map/all_to_all | solution.py:392
  148.9 13.8 %collective-permute-start.18 = (bf16[512,1152]{1,0:T(8,128)(2,1)}, bf16[512,1152]{1,0:T(8,128)(2,1)}, u32[]{:S(2)}, u32[]{:S(2)}) collective-permute-start(bf16[512,1152]{1,0:T(8,128)(2,1)} %collective-permute-done.15.refs_1_), channel_id=1, source_target_pairs={{0,1},{1,0},{2,3},{3,2},{4,5},{5,4},{6,7},{7,6},{8,9},{9,8},{10,11... | collective-permute-start | bytes 3538952 | tf_op jit(solution)/shard_map/ppermute | solution.py:272
  149.5 13.1 %collective-permute-start.19 = (bf16[512,1152]{1,0:T(8,128)(2,1)}, bf16[512,1152]{1,0:T(8,128)(2,1)}, u32[]{:S(2)}, u32[]{:S(2)}) collective-permute-start(bf16[512,1152]{1,0:T(8,128)(2,1)} %collective-permute-done.16.refs_2_), channel_id=1, source_target_pairs={{0,1},{1,0},{2,3},{3,2},{4,5},{5,4},{6,7},{7,6},{8,9},{9,8},{10,11... | collective-permute-start | bytes 3538952 | tf_op jit(solution)/shard_map/ppermute | solution.py:272
Sparse Core Ops, SparseCore 0:
  15.6 52.7 all-gather.2
  70.3 40.2 all-gather.4

commit v2 on v1

--- a/solution.py
+++ b/solution.py
@@ -384,7 +384,7 @@
         ],
         any_in=(0, 1, 3, 4, 5, 6, 7, 8),
         any_out=(0,),
-        mib=60,
+        mib=48,
         us=4,
     )(o_s, clip.reshape(320, D), modulation, *proj, *proj_other)
     _, tq[0] = lax.optimization_barrier((chunks, tq[0]))

time: 219 us -> 222 us (1.014)
  local copies, waits for them, and re-layouts: 13.1 us -> 19.5 us
    unnamed x26 -> x42, local copies, waits for them, and re-layouts: 7.34 us -> 13.7 us
    all_to_all x1, waiting for transfers between devices: 13.1 us -> 17.2 us  [on_device(): chunks = lax.all_to_all(chunks, 'frame', 0, 0, tiled=True)]
    ppermute x4, waiting for transfers between devices: 10.6 us -> 6.52 us  [from_y_neighbours(): got.append(lax.ppermute(part, ('frame', 'row'), pairs))]
  transfers between devices with their start and end apart: 26 -> 26, of which waited for: 11 -> 11; matrix products, arithmetic and copies ran while one was open for 3% -> 3% of each run, Pallas kernels for 13% -> 12%
where the time goes in v2:
time: 222 us; the launch traced here: 221 us
  waiting for transfers between devices  68.1 us (31%)
  Pallas kernels  45.9 us (21%)
  starting transfers between devices  45.2 us (20%)
  blocking collectives  28.9 us (13%)
  local copies, waits for them, and re-layouts  19.5 us (9%)
  between operations  13.6 us (6%)
    all_to_all x1, blocking collectives, on_device(): o_t = lax.all_to_all(o_t, 'frame', 0, 0, tiled=True)  28.9 us
    ppermute x6, waiting for transfers between devices, shift_x(): return lax.ppermute(value, 'row', pairs)  21 us
    pallas_call x1, Pallas kernels, on_device(): call(spatial_kernel, sds((16, tokens, GROUP)), 10, scratch=[pltpu.VMEM((1...  17.7 us
    all_to_all x1, waiting for transfers between devices, on_device(): chunks = lax.all_to_all(chunks, 'frame', 0, 0, tiled=True)  17.2 us
    pallas_call x1, Pallas kernels, on_device(): call(temporal_kernel, sds((16, 24, D)), 7, scratch=[pltpu.VMEM((2, 2, 320...  14 us
    unnamed x42, local copies, waits for them, and re-layouts  13.7 us
    all_to_all x1, waiting for transfers between devices, on_device(): lax.all_to_all(first.reshape(16, 36, 216), 'frame', 0, 0, tiled=True)  10.8 us
    all_to_all x1, starting transfers between devices, on_device(): lax.all_to_all(first.reshape(16, 36, 216), 'frame', 0, 0, tiled=True)  8.7 us
  transfers between devices with their start and end apart: 26, of which 11 were waited for; matrix products, arithmetic and copies ran while one was open for 3% of the time, Pallas kernels for 12%

profile of v2, /device:TPU:32, one launch (start us, length us, event | category | flops | bytes accessed | tf_op | source)
XLA Modules:
  0.0 221.3 jit_solution(11355834672734180794)
XLA Ops:
  6.5 1.0 copy-done
  7.6 0.2 constant_dynamic-slice_fusion
  7.7 0.0 copy-start.5
  7.7 1.1 copy-done.5
  8.8 0.8 copy-done.16
  9.6 0.5 shard_map.64
  10.2 0.1 collective-permute-start
  10.3 3.3 %collective-permute-start.3 = (bf16[2,80,1152]{2,1,0:T(8,128)(2,1)S(1)}, bf16[2,80,1152]{2,1,0:T(8,128)(2,1)S(1)}, u32[]{:S(2)}, u32[]{:S(2)}) collective-permute-start(bf16[2,80,1152]{2,1,0:T(8,128)(2,1)S(1)} %get-tuple-element.45), channel_id=1, source_target_pairs={{0,8},{1,9},{2,10},{3,11},{4,12},{5,13},{6,14},{7,15},{8,0},{9,1},... | collective-permute-start | bytes 1105928 | tf_op jit(solution)/shard_map/ppermute | solution.py:276
  13.5 2.0 shard_map.67
  15.5 0.0 all-gather.3.cloned.1.call-update
  15.6 0.2 copy.8
  15.8 0.8 reshape.10
  16.5 8.7 %all-to-all-start = ((bf16[16,36,216]{2,1,0:T(8,128)(2,1)}), bf16[16,36,216]{2,1,0:T(8,128)(2,1)S(1)}, u32[]{:S(2)}, u32[]{:S(2)}) async-start(bf16[16,36,216]{2,1,0:T(8,128)(2,1)} %reshape.10), calls=%async_computation | async-start | bytes 655360 | tf_op jit(solution)/shard_map/all_to_all | solution.py:330
  25.2 0.0 collective-permute-done.3
  25.3 0.1 collective-permute-start.4
  25.4 2.8 %collective-permute-start.2 = (bf16[160,1152]{1,0:T(8,128)(2,1)S(1)}, bf16[160,1152]{1,0:T(8,128)(2,1)S(1)}, u32[]{:S(2)}, u32[]{:S(2)}) collective-permute-start(bf16[160,1152]{1,0:T(8,128)(2,1)S(1)} %pad_maximum_fusion.refs_0_), channel_id=1, source_target_pairs={{0,6},{1,7},{2,0},{3,1},{4,2},{5,3},{6,4},{7,5},{8,14},{9,15},{10,... | collective-permute-start | bytes 1105928 | tf_op jit(solution)/shard_map/ppermute | solution.py:268
  28.3 10.8 %all-to-all-done.w_ref = bf16[16,36,216]{2,1,0:T(8,128)(2,1)S(1)} async-done(((bf16[16,36,216]{2,1,0:T(8,128)(2,1)}), bf16[16,36,216]{2,1,0:T(8,128)(2,1)S(1)}, u32[]{:S(2)}, u32[]{:S(2)}) %all-to-all-start) | async-done | bytes 248864 | tf_op jit(solution)/shard_map/all_to_all | solution.py:330
  39.0 1.2 shard_map.65
  40.3 0.0 collective-permute-done.1.refs_2_
  40.3 8.0 %all-to-all-start.1 = ((bf16[16,40,864]{2,1,0:T(8,128)(2,1)}), bf16[16,40,864]{2,1,0:T(8,128)(2,1)}, u32[]{:S(2)}, u32[]{:S(2)}) async-start(bf16[16,40,864]{2,1,0:T(8,128)(2,1)} %shard_map.65), calls=%async_computation.1 | async-start | bytes 2293760 | tf_op jit(solution)/shard_map/all_to_all | solution.py:340
  48.2 0.0 all-gather.5.cloned.1.call-start
  48.3 0.7 all-gather.5.cloned.1.call-update
  49.0 0.8 collective-permute-start.5
  49.8 1.1 collective-permute-start.8
  51.0 1.6 collective-permute-start.7
  52.6 1.4 collective-permute-start.6
  54.0 8.2 %collective-permute-done.5.refs_4_ = bf16[160,1152]{1,0:T(8,128)(2,1)S(1)} collective-permute-done((bf16[160,1152]{1,0:T(8,128)(2,1)S(1)}, bf16[160,1152]{1,0:T(8,128)(2,1)S(1)}, u32[]{:S(2)}, u32[]{:S(2)}) %collective-permute-start.5) | collective-permute-done | bytes 368672 | tf_op jit(solution)/shard_map/ppermute | solution.py:268
  62.2 5.6 %collective-permute-done.8.refs_7_ = bf16[160,1152]{1,0:T(8,128)(2,1)S(1)} collective-permute-done((bf16[160,1152]{1,0:T(8,128)(2,1)S(1)}, bf16[160,1152]{1,0:T(8,128)(2,1)S(1)}, u32[]{:S(2)}, u32[]{:S(2)}) %collective-permute-start.8) | collective-permute-done | bytes 368672 | tf_op jit(solution)/shard_map/ppermute | solution.py:268
  67.8 2.2 collective-permute-done.7.refs_5_
  70.1 0.8 copy-done.20
  70.8 4.9 %collective-permute-done.6.refs_3_ = bf16[160,1152]{1,0:T(8,128)(2,1)S(1)} collective-permute-done((bf16[160,1152]{1,0:T(8,128)(2,1)S(1)}, bf16[160,1152]{1,0:T(8,128)(2,1)S(1)}, u32[]{:S(2)}, u32[]{:S(2)}) %collective-permute-start.6) | collective-permute-done | bytes 368672 | tf_op jit(solution)/shard_map/ppermute | solution.py:268
  75.7 3.0 %all-to-all-done.1.refs_8_ = bf16[16,40,864]{2,1,0:T(8,128)(2,1)} async-done(((bf16[16,40,864]{2,1,0:T(8,128)(2,1)}), bf16[16,40,864]{2,1,0:T(8,128)(2,1)}, u32[]{:S(2)}, u32[]{:S(2)}) %all-to-all-start.1) | async-done | bytes 1105952 | tf_op jit(solution)/shard_map/all_to_all | solution.py:340
  78.7 1.4 fusion.1
  80.1 1.8 collective-permute-start.11
  81.9 0.0 collective-permute-start.10
  81.9 1.0 copy-done.13
  82.9 1.0 copy-done.15
  83.9 17.7 %shard_map.66 = bf16[16,80,288]{2,1,0:T(8,128)(2,1)} custom-call(bf16[160,1152]{1,0:T(8,128)(2,1)S(1)} %pad_maximum_fusion.refs_0_, bf16[160,1152]{1,0:T(8,128)(2,1)S(1)} %pad_maximum_fusion.1.refs_1_, bf16[160,1152]{1,0:T(8,128)(2,1)S(1)} %collective-permute-done.1.refs_2_, bf16[160,1152]{1,0:T(8,128)(2,1)S(1)} %copy-done.15, ...), custom_call_target="tpu_custom_call" | custom-call | flops 15000000512 | bytes 15000000 | tf_op jit(solution)/shard_map/pallas_call | solution.py:346
  101.7 0.3 collective-permute-start.12
  102.0 6.3 %all-to-all-start.2 = ((bf16[16,80,288]{2,1,0:T(8,128)(2,1)}), bf16[16,80,288]{2,1,0:T(8,128)(2,1)S(1)}, u32[]{:S(2)}, u32[]{:S(2)}) async-start(bf16[16,80,288]{2,1,0:T(8,128)(2,1)} %shard_map.66), calls=%async_computation.2 | async-start | bytes 1966080 | tf_op jit(solution)/shard_map/all_to_all | solution.py:368
  108.3 0.4 collective-permute-start.13
  108.7 0.2 collective-permute-start.14
  108.9 1.7 all-gather.5.cloned.1.call-done.refs_0_
  110.6 3.2 %fusion = (bf16[512,1152]{1,0:T(8,128)(2,1)}, bf16[512,1152]{1,0:T(8,128)(2,1)}) fusion(bf16[1024,1152]{1,0:T(8,128)(2,1)} %all-gather.5.cloned.1.call-done.refs_0_), kind=kLoop, calls=%fused_computation.5 | loop fusion | bytes 4718592 | tf_op jit(solution)/shard_map/slice | solution.py:281
  113.8 1.6 collective-permute-start.15
  115.4 2.1 collective-permute-start.16
  117.5 0.9 copy-done.10
  118.4 7.2 %all-to-all-done.2.o_in = bf16[16,80,288]{2,1,0:T(8,128)(2,1)S(1)} async-done(((bf16[16,80,288]{2,1,0:T(8,128)(2,1)}), bf16[16,80,288]{2,1,0:T(8,128)(2,1)S(1)}, u32[]{:S(2)}, u32[]{:S(2)}) %all-to-all-start.2) | async-done | bytes 737312 | tf_op jit(solution)/shard_map/all_to_all | solution.py:368
  125.6 1.0 copy-done.2
  126.6 1.2 copy-done.3
  127.8 1.1 copy-done.6
  128.9 1.1 copy-done.9
  130.0 1.1 copy-done.11
  131.1 0.8 copy-done.17
  131.8 5.0 %shard_map.68 = (f32[320,1152]{1,0:T(8,128)}, bf16[16,24,1152]{2,1,0:T(8,128)(2,1)S(1)}) custom-call(bf16[16,80,288]{2,1,0:T(8,128)(2,1)S(1)} %copy-done.3, bf16[320,1152]{1,0:T(8,128)(2,1)S(1)} %bitcast.11, f32[6,1152]{1,0:T(8,128)S(1)} %copy-done.17, bf16[576,1152]{1,0:T(8,128)(2,1)} %all-gather.3.cloned.1.call-done.m0, bf16[288,1152]{1,0:T(8,128)(2,1)S(1)} %copy-done.9, ...), custom_call_target="tpu_custom_call" | custom-call | flops 4000000000 | bytes 4000000 | tf_op jit(solution)/shard_map/pallas_call | solution.py:373
  136.8 0.9 copy-done.4
  137.8 4.5 %all-to-all-start.3 = ((bf16[16,24,1152]{2,1,0:T(8,128)(2,1)}), bf16[16,24,1152]{2,1,0:T(8,128)(2,1)}, u32[]{:S(2)}, u32[]{:S(2)}) async-start(bf16[16,24,1152]{2,1,0:T(8,128)(2,1)} %copy-done.4), calls=%async_computation.3 | async-start | bytes 1769472 | tf_op jit(solution)/shard_map/all_to_all | solution.py:392
  142.3 3.5 %collective-permute-done.15.refs_1_ = bf16[512,1152]{1,0:T(8,128)(2,1)} collective-permute-done((bf16[512,1152]{1,0:T(8,128)(2,1)}, bf16[512,1152]{1,0:T(8,128)(2,1)}, u32[]{:S(2)}, u32[]{:S(2)}) %collective-permute-start.15) | collective-permute-done | bytes 1179680 | tf_op jit(solution)/shard_map/ppermute | solution.py:288
  145.8 3.0 %collective-permute-done.16.refs_2_ = bf16[512,1152]{1,0:T(8,128)(2,1)} collective-permute-done((bf16[512,1152]{1,0:T(8,128)(2,1)}, bf16[512,1152]{1,0:T(8,128)(2,1)}, u32[]{:S(2)}, u32[]{:S(2)}) %collective-permute-start.16) | collective-permute-done | bytes 1179680 | tf_op jit(solution)/shard_map/ppermute | solution.py:288
  148.8 0.0 collective-permute-start.19
  148.8 17.2 %all-to-all-done.3.x_ref = bf16[16,24,1152]{2,1,0:T(8,128)(2,1)} async-done(((bf16[16,24,1152]{2,1,0:T(8,128)(2,1)}), bf16[16,24,1152]{2,1,0:T(8,128)(2,1)}, u32[]{:S(2)}, u32[]{:S(2)}) %all-to-all-start.3) | async-done | bytes 884768 | tf_op jit(solution)/shard_map/all_to_all | solution.py:392
  166.0 14.0 %shard_map.69 = bf16[16,24,1152]{2,1,0:T(8,128)(2,1)S(1)} custom-call(bf16[16,24,1152]{2,1,0:T(8,128)(2,1)} %all-to-all-done.3.x_ref, bf16[1024,1152]{1,0:T(8,128)(2,1)S(1)} %copy-done.1, bf16[512,1152]{1,0:T(8,128)(2,1)} %collective-permute-done.15.refs_1_, bf16[512,1152]{1,0:T(8,128)(2,1)} %collective-permute-done.16.refs_2_, ...), custom_call_target="tpu_custom_call" | custom-call | flops 12000000000 | bytes 12000000 | tf_op jit(solution)/shard_map/pallas_call | solution.py:394
  180.0 28.9 %all_to_all.25.o_in = bf16[16,24,1152]{2,1,0:T(8,128)(2,1)} all-to-all(bf16[16,24,1152]{2,1,0:T(8,128)(2,1)S(1)} %shard_map.69), channel_id=1, replica_groups=mesh['frame'=16,'row'=16] {'frame'}, dimensions={0} | all-to-all | bytes 1769472 | tf_op jit(solution)/shard_map/all_to_all | solution.py:402
  208.9 5.5 %shard_map.70 = bf16[320,1152]{1,0:T(8,128)(2,1)} custom-call(bf16[16,24,1152]{2,1,0:T(8,128)(2,1)} %all_to_all.25.o_in, f32[320,1152]{1,0:T(8,128)} %get-tuple-element.70.mid_in, f32[6,1152]{1,0:T(8,128)} %mod_ref.5, bf16[576,1152]{1,0:T(8,128)(2,1)} %all-gather.3.cloned.1.call-done.m0, bf16[288,1152]{1,0:T(8,128)(2,1)} %copy-done.8, ...), custom_call_target="tpu_custom_call" | custom-call | flops 4000000000 | bytes 4000000 | tf_op jit(solution)/shard_map/pallas_call | solution.py:403
  (48 shorter events, 0.2 us)
Async XLA Ops:
  6.5 1.0 copy-start
  6.5 72.2 %all-gather.3.cloned.1.call-start = ((), (), s32[]{:S(2)}) async-start(), calls=%async_computation.5 | async-start | bytes 1492992 | tf_op jit(solution)/shard_map/all_gather | solution.py:294
  7.7 1.1 copy-start.5
  8.8 0.8 copy-start.16
  10.2 5.4 %collective-permute-start = (bf16[80,1152]{1,0:T(8,128)(2,1)S(1)}, bf16[80,1152]{1,0:T(8,128)(2,1)S(1)}, u32[]{:S(2)}, u32[]{:S(2)}) collective-permute-start(bf16[80,1152]{1,0:T(8,128)(2,1)S(1)} %get-tuple-element.42), channel_id=1, source_target_pairs={{0,1},{1,0},{2,3},{3,2},{4,5},{5,4},{6,7},{7,6},{8,9},{9,8},{10,11... | collective-permute-start | bytes 552968 | tf_op jit(solution)/shard_map/ppermute | solution.py:272
  10.3 15.0 %collective-permute-start.3 = (bf16[2,80,1152]{2,1,0:T(8,128)(2,1)S(1)}, bf16[2,80,1152]{2,1,0:T(8,128)(2,1)S(1)}, u32[]{:S(2)}, u32[]{:S(2)}) collective-permute-start(bf16[2,80,1152]{2,1,0:T(8,128)(2,1)S(1)} %get-tuple-element.45), channel_id=1, source_target_pairs={{0,8},{1,9},{2,10},{3,11},{4,12},{5,13},{6,14},{7,15},{8,0},{9,1},... | collective-permute-start | bytes 1105928 | tf_op jit(solution)/shard_map/ppermute | solution.py:276
  16.5 22.5 %all-to-all-start = ((bf16[16,36,216]{2,1,0:T(8,128)(2,1)}), bf16[16,36,216]{2,1,0:T(8,128)(2,1)S(1)}, u32[]{:S(2)}, u32[]{:S(2)}) async-start(bf16[16,36,216]{2,1,0:T(8,128)(2,1)} %reshape.10), calls=%async_computation | async-start | bytes 655360 | tf_op jit(solution)/shard_map/all_to_all | solution.py:330
  25.3 2.9 %collective-permute-start.4 = (bf16[80,1152]{1,0:T(8,128)(2,1)S(1)}, bf16[80,1152]{1,0:T(8,128)(2,1)S(1)}, u32[]{:S(2)}, u32[]{:S(2)}) collective-permute-start(bf16[80,1152]{1,0:T(8,128)(2,1)S(1)} %get-tuple-element.76), channel_id=1, source_target_pairs={{0,1},{1,0},{2,3},{3,2},{4,5},{5,4},{6,7},{7,6},{8,9},{9,8},{10,11... | collective-permute-start | bytes 552968 | tf_op jit(solution)/shard_map/ppermute | solution.py:272
  25.4 14.9 %collective-permute-start.2 = (bf16[160,1152]{1,0:T(8,128)(2,1)S(1)}, bf16[160,1152]{1,0:T(8,128)(2,1)S(1)}, u32[]{:S(2)}, u32[]{:S(2)}) collective-permute-start(bf16[160,1152]{1,0:T(8,128)(2,1)S(1)} %pad_maximum_fusion.refs_0_), channel_id=1, source_target_pairs={{0,6},{1,7},{2,0},{3,1},{4,2},{5,3},{6,4},{7,5},{8,14},{9,15},{10,... | collective-permute-start | bytes 1105928 | tf_op jit(solution)/shard_map/ppermute | solution.py:268
  28.2 12.0 %collective-permute-start.1 = (bf16[160,1152]{1,0:T(8,128)(2,1)S(1)}, bf16[160,1152]{1,0:T(8,128)(2,1)S(1)}, u32[]{:S(2)}, u32[]{:S(2)}) collective-permute-start(bf16[160,1152]{1,0:T(8,128)(2,1)S(1)} %pad_maximum_fusion.refs_0_), channel_id=1, source_target_pairs={{0,2},{1,3},{2,4},{3,5},{4,6},{5,7},{6,0},{7,1},{8,10},{9,11},{10,... | collective-permute-start | bytes 1105928 | tf_op jit(solution)/shard_map/ppermute | solution.py:268
  40.3 8.7 %copy-start.18 = (bf16[160,1152]{1,0:T(8,128)(2,1)}, bf16[160,1152]{1,0:T(8,128)(2,1)S(1)}, u32[]{:S(2)}) copy-start(bf16[160,1152]{1,0:T(8,128)(2,1)S(1)} %collective-permute-done.2.refs_6_) | copy-start | bytes 1105924
  40.3 38.5 %all-to-all-start.1 = ((bf16[16,40,864]{2,1,0:T(8,128)(2,1)}), bf16[16,40,864]{2,1,0:T(8,128)(2,1)}, u32[]{:S(2)}, u32[]{:S(2)}) async-start(bf16[16,40,864]{2,1,0:T(8,128)(2,1)} %shard_map.65), calls=%async_computation.1 | async-start | bytes 2293760 | tf_op jit(solution)/shard_map/all_to_all | solution.py:340
  48.2 62.4 %all-gather.5.cloned.1.call-start = ((), (), s32[]{:S(2)}) async-start(), calls=%async_computation.6 | async-start | bytes 2654208 | tf_op jit(solution)/shard_map/all_gather | solution.py:294
  49.0 13.2 %collective-permute-start.5 = (bf16[160,1152]{1,0:T(8,128)(2,1)S(1)}, bf16[160,1152]{1,0:T(8,128)(2,1)S(1)}, u32[]{:S(2)}, u32[]{:S(2)}) collective-permute-start(bf16[160,1152]{1,0:T(8,128)(2,1)S(1)} %pad_maximum_fusion.refs_0_), channel_id=1, source_target_pairs={{0,4},{1,5},{2,6},{3,7},{4,0},{5,1},{6,2},{7,3},{8,12},{9,13},{10,... | collective-permute-start | bytes 1105928 | tf_op jit(solution)/shard_map/ppermute | solution.py:268
  49.8 18.0 %collective-permute-start.8 = (bf16[160,1152]{1,0:T(8,128)(2,1)S(1)}, bf16[160,1152]{1,0:T(8,128)(2,1)S(1)}, u32[]{:S(2)}, u32[]{:S(2)}) collective-permute-start(bf16[160,1152]{1,0:T(8,128)(2,1)S(1)} %pad_maximum_fusion.1.refs_1_), channel_id=1, source_target_pairs={{0,6},{1,7},{2,0},{3,1},{4,2},{5,3},{6,4},{7,5},{8,14},{9,15},{10,... | collective-permute-start | bytes 1105928 | tf_op jit(solution)/shard_map/ppermute | solution.py:268
  51.0 19.1 %collective-permute-start.7 = (bf16[160,1152]{1,0:T(8,128)(2,1)S(1)}, bf16[160,1152]{1,0:T(8,128)(2,1)S(1)}, u32[]{:S(2)}, u32[]{:S(2)}) collective-permute-start(bf16[160,1152]{1,0:T(8,128)(2,1)S(1)} %pad_maximum_fusion.1.refs_1_), channel_id=1, source_target_pairs={{0,4},{1,5},{2,6},{3,7},{4,0},{5,1},{6,2},{7,3},{8,12},{9,13},{10,... | collective-permute-start | bytes 1105928 | tf_op jit(solution)/shard_map/ppermute | solution.py:268
  52.6 23.1 %collective-permute-start.6 = (bf16[160,1152]{1,0:T(8,128)(2,1)S(1)}, bf16[160,1152]{1,0:T(8,128)(2,1)S(1)}, u32[]{:S(2)}, u32[]{:S(2)}) collective-permute-start(bf16[160,1152]{1,0:T(8,128)(2,1)S(1)} %pad_maximum_fusion.1.refs_1_), channel_id=1, source_target_pairs={{0,2},{1,3},{2,4},{3,5},{4,6},{5,7},{6,0},{7,1},{8,10},{9,11},{10,... | collective-permute-start | bytes 1105928 | tf_op jit(solution)/shard_map/ppermute | solution.py:268
  62.2 17.9 %copy-start.12 = (bf16[160,1152]{1,0:T(8,128)(2,1)}, bf16[160,1152]{1,0:T(8,128)(2,1)S(1)}, u32[]{:S(2)}) copy-start(bf16[160,1152]{1,0:T(8,128)(2,1)S(1)} %collective-permute-done.5.refs_4_) | copy-start | bytes 1105924
  67.8 2.2 copy-start.19
  70.0 0.8 copy-start.20
  75.7 4.4 %copy-start.14 = (bf16[160,1152]{1,0:T(8,128)(2,1)}, bf16[160,1152]{1,0:T(8,128)(2,1)S(1)}, u32[]{:S(2)}) copy-start(bf16[160,1152]{1,0:T(8,128)(2,1)S(1)} %collective-permute-done.6.refs_3_) | copy-start | bytes 1105924
  78.7 3.2 %collective-permute-start.9 = (bf16[16,40,864]{2,1,0:T(8,128)(2,1)}, bf16[16,40,864]{2,1,0:T(8,128)(2,1)}, u32[]{:S(2)}, u32[]{:S(2)}) collective-permute-start(bf16[16,40,864]{2,1,0:T(8,128)(2,1)} %all-to-all-done.1.refs_8_), channel_id=1, source_target_pairs={{0,1},{1,0},{2,3},{3,2},{4,5},{5,4},{6,7},{7,6},{8,9},{9,8},{10,11... | collective-permute-start | bytes 3317768 | tf_op jit(solution)/shard_map/ppermute | solution.py:272
  80.1 21.5 %collective-permute-start.11 = (bf16[288,1152]{1,0:T(8,128)(2,1)S(1)}, bf16[288,1152]{1,0:T(8,128)(2,1)S(1)}, u32[]{:S(2)}, u32[]{:S(2)}) collective-permute-start(bf16[288,1152]{1,0:T(8,128)(2,1)S(1)} %get-tuple-element.73), channel_id=1, source_target_pairs={{0,136},{1,137},{2,138},{3,139},{4,140},{5,141},{6,142},{7,143},{8... | collective-permute-start | bytes 1990664 | tf_op jit(solution)/shard_map/ppermute | solution.py:288
  81.9 19.7 %collective-permute-start.10 = (bf16[288,1152]{1,0:T(8,128)(2,1)S(1)}, bf16[288,1152]{1,0:T(8,128)(2,1)S(1)}, u32[]{:S(2)}, u32[]{:S(2)}) collective-permute-start(bf16[288,1152]{1,0:T(8,128)(2,1)S(1)} %get-tuple-element.74), channel_id=1, source_target_pairs={{0,128},{1,129},{2,130},{3,131},{4,132},{5,133},{6,134},{7,135},{8... | collective-permute-start | bytes 1990664 | tf_op jit(solution)/shard_map/ppermute | solution.py:288
  81.9 1.0 copy-start.13
  82.9 1.0 copy-start.15
  101.7 24.9 %copy-start.7 = (bf16[288,1152]{1,0:T(8,128)(2,1)}, bf16[288,1152]{1,0:T(8,128)(2,1)S(1)}, u32[]{:S(2)}) copy-start(bf16[288,1152]{1,0:T(8,128)(2,1)S(1)} %collective-permute-done.11.m2) | copy-start | bytes 1990660
  101.7 12.1 %copy-start.8 = (bf16[288,1152]{1,0:T(8,128)(2,1)}, bf16[288,1152]{1,0:T(8,128)(2,1)S(1)}, u32[]{:S(2)}) copy-start(bf16[288,1152]{1,0:T(8,128)(2,1)S(1)} %collective-permute-done.10.m1) | copy-start | bytes 1990660
  101.7 12.1 %collective-permute-start.12 = (bf16[576,1152]{1,0:T(8,128)(2,1)}, bf16[576,1152]{1,0:T(8,128)(2,1)}, u32[]{:S(2)}, u32[]{:S(2)}) collective-permute-start(bf16[576,1152]{1,0:T(8,128)(2,1)} %all-gather.3.cloned.1.call-done.m0), channel_id=1, source_target_pairs={{0,1},{1,0},{2,3},{3,2},{4,5},{5,4},{6,7},{7,6},{8,9},{9,8},{10,11... | collective-permute-start | bytes 3981320 | tf_op jit(solution)/shard_map/ppermute | solution.py:272
  102.0 23.6 %all-to-all-start.2 = ((bf16[16,80,288]{2,1,0:T(8,128)(2,1)}), bf16[16,80,288]{2,1,0:T(8,128)(2,1)S(1)}, u32[]{:S(2)}, u32[]{:S(2)}) async-start(bf16[16,80,288]{2,1,0:T(8,128)(2,1)} %shard_map.66), calls=%async_computation.2 | async-start | bytes 1966080 | tf_op jit(solution)/shard_map/all_to_all | solution.py:368
  108.3 9.3 %collective-permute-start.13 = (bf16[288,1152]{1,0:T(8,128)(2,1)S(1)}, bf16[288,1152]{1,0:T(8,128)(2,1)S(1)}, u32[]{:S(2)}, u32[]{:S(2)}) collective-permute-start(bf16[288,1152]{1,0:T(8,128)(2,1)S(1)} %collective-permute-done.10.m1), channel_id=1, source_target_pairs={{0,1},{1,0},{2,3},{3,2},{4,5},{5,4},{6,7},{7,6},{8,9},{9,8},{10,11... | collective-permute-start | bytes 1990664 | tf_op jit(solution)/shard_map/ppermute | solution.py:272
  108.7 9.7 %collective-permute-start.14 = (bf16[288,1152]{1,0:T(8,128)(2,1)S(1)}, bf16[288,1152]{1,0:T(8,128)(2,1)}, u32[]{:S(2)}, u32[]{:S(2)}) collective-permute-start(bf16[288,1152]{1,0:T(8,128)(2,1)S(1)} %collective-permute-done.11.m2), channel_id=1, source_target_pairs={{0,1},{1,0},{2,3},{3,2},{4,5},{5,4},{6,7},{7,6},{8,9},{9,8},{10,11... | collective-permute-start | bytes 1990664 | tf_op jit(solution)/shard_map/ppermute | solution.py:272
  113.8 32.0 %collective-permute-start.15 = (bf16[512,1152]{1,0:T(8,128)(2,1)}, bf16[512,1152]{1,0:T(8,128)(2,1)}, u32[]{:S(2)}, u32[]{:S(2)}) collective-permute-start(bf16[512,1152]{1,0:T(8,128)(2,1)} %get-tuple-element.68), channel_id=1, source_target_pairs={{0,128},{1,129},{2,130},{3,131},{4,132},{5,133},{6,134},{7,135},{8... | collective-permute-start | bytes 3538952 | tf_op jit(solution)/shard_map/ppermute | solution.py:288
  115.4 33.4 %collective-permute-start.16 = (bf16[512,1152]{1,0:T(8,128)(2,1)}, bf16[512,1152]{1,0:T(8,128)(2,1)}, u32[]{:S(2)}, u32[]{:S(2)}) collective-permute-start(bf16[512,1152]{1,0:T(8,128)(2,1)} %get-tuple-element.69), channel_id=1, source_target_pairs={{0,136},{1,137},{2,138},{3,139},{4,140},{5,141},{6,142},{7,143},{8... | collective-permute-start | bytes 3538952 | tf_op jit(solution)/shard_map/ppermute | solution.py:288
  117.5 0.9 copy-start.10
  125.6 1.0 copy-start.2
  126.6 1.2 copy-start.3
  127.8 1.1 copy-start.6
  128.9 1.1 copy-start.9
  130.0 1.1 copy-start.11
  131.1 0.8 copy-start.17
  131.8 6.0 %copy-start.1 = (bf16[1024,1152]{1,0:T(8,128)(2,1)S(1)}, bf16[1024,1152]{1,0:T(8,128)(2,1)}, u32[]{:S(2)}) copy-start(bf16[1024,1152]{1,0:T(8,128)(2,1)} %all-gather.5.cloned.1.call-done.refs_0_) | copy-start | bytes 7077892
  136.8 1.0 copy-start.4
  137.8 28.2 %collective-permute-start.17 = (bf16[1024,1152]{1,0:T(8,128)(2,1)S(1)}, bf16[1024,1152]{1,0:T(8,128)(2,1)}, u32[]{:S(2)}, u32[]{:S(2)}) collective-permute-start(bf16[1024,1152]{1,0:T(8,128)(2,1)S(1)} %copy-done.1), channel_id=1, source_target_pairs={{0,1},{1,0},{2,3},{3,2},{4,5},{5,4},{6,7},{7,6},{8,9},{9,8},{10,11... | collective-permute-start | bytes 7077896 | tf_op jit(solution)/shard_map/ppermute | solution.py:272
  137.8 28.2 %all-to-all-start.3 = ((bf16[16,24,1152]{2,1,0:T(8,128)(2,1)}), bf16[16,24,1152]{2,1,0:T(8,128)(2,1)}, u32[]{:S(2)}, u32[]{:S(2)}) async-start(bf16[16,24,1152]{2,1,0:T(8,128)(2,1)} %copy-done.4), calls=%async_computation.3 | async-start | bytes 1769472 | tf_op jit(solution)/shard_map/all_to_all | solution.py:392
  145.8 20.2 %collective-permute-start.18 = (bf16[512,1152]{1,0:T(8,128)(2,1)}, bf16[512,1152]{1,0:T(8,128)(2,1)}, u32[]{:S(2)}, u32[]{:S(2)}) collective-permute-start(bf16[512,1152]{1,0:T(8,128)(2,1)} %collective-permute-done.15.refs_1_), channel_id=1, source_target_pairs={{0,1},{1,0},{2,3},{3,2},{4,5},{5,4},{6,7},{7,6},{8,9},{9,8},{10,11... | collective-permute-start | bytes 3538952 | tf_op jit(solution)/shard_map/ppermute | solution.py:272
  148.8 17.2 %collective-permute-start.19 = (bf16[512,1152]{1,0:T(8,128)(2,1)}, bf16[512,1152]{1,0:T(8,128)(2,1)}, u32[]{:S(2)}, u32[]{:S(2)}) collective-permute-start(bf16[512,1152]{1,0:T(8,128)(2,1)} %collective-permute-done.16.refs_2_), channel_id=1, source_target_pairs={{0,1},{1,0},{2,3},{3,2},{4,5},{5,4},{6,7},{7,6},{8,9},{9,8},{10,11... | collective-permute-start | bytes 3538952 | tf_op jit(solution)/shard_map/ppermute | solution.py:272
Sparse Core Ops, SparseCore 0:
  15.7 52.7 all-gather.2
  70.3 40.2 all-gather.4
